TPU v7x, 32 devices: a whole 2x2x4 slice. The times are simulated.
32 devices in a mesh: walker: 4 (over y, x), tangent: 4 (over z), feat: 2 (over core).
Axes of the slice: x: 2, y: 2, z: 4, core: 2. Of those that a mesh axis runs over, the one named last changes fastest.
Arguments:
- value_in: bfloat16 [128, 512], P('walker', 'feat'), may hold values from -0.94921875 to 0.94921875
- tang_in: bfloat16 [128, 768, 512], P('walker', 'tangent', 'feat'), may hold values from -1.01 to 1.01
- lap_in: bfloat16 [128, 512], P('walker', 'feat'), may hold values from -6 to 6
- w_first: bfloat16 [512, 512], P(('walker', 'tangent', 'feat')), may hold values from -0.25 to 0.25
- b_first: float32 [512], replicated, may hold values from -3 to 3
- w_second: bfloat16 [512, 512], P(('walker', 'tangent', 'feat')), may hold values from -0.25 to 0.25
- b_second: float32 [512], replicated, may hold values from -3 to 3
- readout: float32 [512], replicated, may hold values from -0.6 to 0.6
Outputs:
- log_amplitude: float32 [128], P('walker')
- gradient: float32 [128, 768], P('walker', 'tangent')
- kinetic: float32 [128], P('walker')
All inputs are finite; a program needn't handle non-finite values.
Results may differ from a plain program's by a relative error of at most 0.0044.
Values may be sent and summed in bfloat16 or wider, within the bound.
A program may use at most 64 MiB of HBM per device.

v0:
```python
import jax
import jax.numpy as jnp
from jax import lax
from jax.sharding import PartitionSpec as P


def tanh_layer(value, tangents, laplacian, w_full, bias):
    feat_index = lax.axis_index("feat")
    half_width = value.shape[1]
    count_w, count_t = (tangents.shape[0], tangents.shape[1])
    stacked = jnp.stack([value, laplacian])
    w_rows = lax.dynamic_slice_in_dim(w_full, feat_index * half_width, half_width, 0)
    partial_vl = jnp.einsum("kbd,de->kbe", stacked, w_rows, preferred_element_type=jnp.float32)
    partial_grad = jnp.dot(
        tangents.reshape(count_w * count_t, half_width), w_rows, preferred_element_type=jnp.float32
    ).reshape(count_w, count_t, w_full.shape[1])
    summed, grad_pre = (
        lax.psum_scatter(partial_vl, "feat", scatter_dimension=2, tiled=True),
        lax.psum_scatter(partial_grad, "feat", scatter_dimension=2, tiled=True),
    )
    pre_act = summed[0] + bias
    lap_pre = summed[1]
    hidden = jnp.tanh(pre_act)
    slope = 1.0 - hidden * hidden
    bend = -2.0 * hidden * slope
    return (hidden, slope, bend, grad_pre, lap_pre)


def own_half(vector, half_width):
    return lax.dynamic_slice_in_dim(vector, lax.axis_index("feat") * half_width, half_width, 0)


def per_device(value_in, tang_in, lap_in, w_first, b_first, w_second, b_second, readout):
    full_first, full_second = (
        lax.all_gather(w_first, ("walker", "tangent", "feat"), axis=0, tiled=True),
        lax.all_gather(w_second, ("walker", "tangent", "feat"), axis=0, tiled=True),
    )
    half_width = value_in.shape[1]
    value_start, lap_start, tangents_in = (value_in, lap_in, tang_in)
    bias_one = own_half(b_first, half_width)
    bias_two = own_half(b_second, half_width)
    read_weights = own_half(readout, half_width)
    hidden, slope, bend, grad_pre, lap_pre = tanh_layer(
        value_start, tangents_in, lap_start, full_first, bias_one
    )
    curv_first = lax.psum(jnp.sum(grad_pre * grad_pre, axis=1), "tangent")
    value_two = hidden.astype(jnp.bfloat16)
    tang_two = (slope[:, None, :] * grad_pre).astype(jnp.bfloat16)
    lap_two = (slope * lap_pre + bend * curv_first).astype(jnp.bfloat16)
    hidden, slope, bend, grad_pre, lap_pre = tanh_layer(
        value_two, tang_two, lap_two, full_second, bias_two
    )
    amp_part = jnp.sum(read_weights * hidden, axis=-1)
    grad_part = jnp.sum(grad_pre * (read_weights * slope)[:, None, :], axis=-1)
    local_squares = jnp.sum(grad_pre * grad_pre, axis=1)
    curv_second = lax.psum(local_squares, "tangent")
    lap_part = jnp.sum(read_weights * (slope * lap_pre + bend * curv_second), axis=-1)
    log_amplitude, gradient, laplace = lax.psum((amp_part, grad_part, lap_part), "feat")
    squares = lax.psum(jnp.sum(gradient * gradient, axis=-1), "tangent")
    kinetic = -0.5 * (laplace + squares)
    return (log_amplitude, gradient, kinetic)


def solution(mesh):
    placed = (
        P("walker", "feat"),
        P("walker", "tangent", "feat"),
        P("walker", "feat"),
        P(("walker", "tangent", "feat"), None),
        P(),
        P(("walker", "tangent", "feat"), None),
        P(),
        P(),
    )
    return jax.shard_map(
        per_device,
        mesh=mesh,
        in_specs=placed,
        out_specs=(P("walker"), P("walker", "tangent"), P("walker")),
        check_vma=False,
    )
```

profile of v0, /device:TPU:0, one launch (start us, length us, event | category | flops | bytes accessed | tf_op | source)
XLA Modules:
  0.0 209.3 jit_solution(18067361180043493473)
XLA Ops:
  7.2 0.0 copy-start
  7.2 0.0 reduce-scatter.5.cloned.1.call-start
  7.2 48.4 %all_gather.6 = bf16[512,512]{1,0:T(8,128)(2,1)} all-gather(bf16[16,512]{1,0:T(8,128)(2,1)} %param.11), channel_id=1, replica_groups=mesh['walker'=4,'tangent'=4,'feat'=2] {'walker','tangent','feat'}, dimensions={0}, use_global_device_ids=true | all-gather | bytes 540672 | tf_op jit(solution)/shard_map/all_gather | solution.py:35
  55.7 1.8 fusion.5
  57.5 0.0 reduce-scatter.5.cloned.1.call-update
  57.5 0.0 reduce-scatter.7.cloned.1.call-start
  57.5 0.0 copy-done
  57.5 7.3 %convolution_bitcast_fusion = f32[6144,512]{0,1:T(8,128)} fusion(bf16[6144,256]{1,0:T(8,128)(2,1)S(1)} %bitcast.61, bf16[512,512]{1,0:T(8,128)(2,1)} %all_gather.6, s32[]{:T(128)S(6)} %select_n.2), kind=kOutput, calls=%fused_computation | convolution fusion | flops 1610612736 | bytes 15990788 | tf_op jit(solution)/shard_map/dot_general | solution.py:14
  64.8 12.6 %copy.12 = f32[6144,512]{1,0:T(8,128)} copy(f32[6144,512]{0,1:T(8,128)} %convolution_bitcast_fusion) | data formatting | bytes 25165824 | tf_op jit(solution)/shard_map/dot_general | solution.py:14
  77.4 0.0 copy-start.5
  77.4 0.0 copy-start.4
  77.4 0.0 reduce-scatter.7.cloned.1.call-update
  77.4 0.0 reduce-scatter.9.cloned.1.call-start
  77.5 0.6 copy-done.5
  78.1 0.1 dynamic_slice.17
  78.2 0.0 copy-done.4
  78.2 41.5 %all_gather.7 = bf16[512,512]{1,0:T(8,128)(2,1)} all-gather(bf16[16,512]{1,0:T(8,128)(2,1)S(1)} %copy-done.4), channel_id=1, replica_groups=mesh['walker'=4,'tangent'=4,'feat'=2] {'walker','tangent','feat'}, dimensions={0}, use_global_device_ids=true | all-gather | bytes 540672 | tf_op jit(solution)/shard_map/all_gather | solution.py:36
  119.6 0.0 reduce-scatter.5.cloned.1.call-done
  119.6 0.0 copy-start.1
  119.6 0.8 tanh_convert_fusion
  120.5 0.0 reduce-scatter.7.cloned.1.call-done
  120.5 3.4 %multiply_reduce_fusion.2 = f32[32,256]{1,0:T(8,128)S(1)} fusion(f32[32,192,256]{2,1,0:T(8,128)} %reduce-scatter.7.cloned.1.call-done), kind=kLoop, calls=%fused_computation.4 | loop fusion | flops 3137536 | bytes 6324224 | tf_op jit(solution)/shard_map/reduce_sum | solution.py:46
  123.9 17.1 %psum.42 = f32[32,256]{1,0:T(8,128)S(1)} all-reduce(f32[32,256]{1,0:T(8,128)S(1)} %multiply_reduce_fusion.2), channel_id=1, replica_groups=mesh['walker'=4,'tangent'=4,'feat'=2] {'tangent'}, use_global_device_ids=true, to_apply=%region_3.0 | all-reduce | flops 8192 | bytes 65536 | tf_op jit(solution)/shard_map/psum | solution.py:46
  141.0 0.0 copy-done.1
  141.0 1.8 fusion.3
  142.8 0.0 reduce-scatter.9.cloned.1.call-update
  142.8 0.0 reduce-scatter.11.cloned.1.call-start
  142.9 9.2 %fusion = f32[32,192,512]{2,1,0:T(8,128)} fusion(f32[32,192,256]{2,1,0:T(8,128)} %reduce-scatter.7.cloned.1.call-done, f32[32,256]{1,0:T(8,128)S(1)} %get-tuple-element.11, bf16[512,512]{1,0:T(8,128)(2,1)} %all_gather.7, s32[]{:T(128)S(6)} %select_n.2), kind=kOutput, calls=%fused_computation.5 | convolution fusion | flops 1613758464 | bytes 19169284 | tf_op jit(solution)/shard_map/dot_general | solution.py:14
  152.1 0.0 copy-start.6
  152.1 0.0 copy-start.7
  152.1 0.0 reduce-scatter.11.cloned.1.call-update
  152.1 0.7 copy-done.6
  152.8 0.1 dynamic_slice.15
  152.8 0.0 copy-done.7
  152.8 0.1 dynamic_slice.19
  152.9 0.0 reduce-scatter.9.cloned.1.call-done
  152.9 0.0 copy-start.2
  152.9 0.8 fusion.27
  153.8 18.1 %reduce-scatter.11.cloned.1.call-done = f32[32,192,256]{2,1,0:T(8,128)} async-done(((f32[32,192,512]{2,1,0:T(8,128)}), f32[32,192,256]{2,1,0:T(8,128)}) %reduce-scatter.11.cloned.1.call-update) | async-done | bytes 6291472 | tf_op jit(solution)/shard_map/reduce_scatter | solution.py:19
  171.9 4.0 %multiply_reduce_fusion = (f32[32,256]{1,0:T(8,128)S(1)}, f32[32,192]{1,0:T(8,128)S(1)}) fusion(f32[32,192,256]{2,1,0:T(8,128)} %reduce-scatter.11.cloned.1.call-done, f32[32,256]{1,0:T(8,128)S(1)} %fusion.27), kind=kLoop, calls=%fused_computation.1 | loop fusion | flops 6277120 | bytes 6381568 | tf_op jit(solution)/shard_map/reduce_sum | solution.py:55
  175.8 3.4 %psum.44 = f32[32,192]{1,0:T(8,128)S(1)} all-reduce(f32[32,192]{1,0:T(8,128)S(1)} %get-tuple-element.4), channel_id=1, replica_groups=mesh['walker'=4,'tangent'=4,'feat'=2] {'feat'}, use_global_device_ids=true, to_apply=%region_9.0 | all-reduce | flops 6144 | bytes 49152 | tf_op jit(solution)/shard_map/psum | solution.py:58
  179.3 0.0 copy-start.3
  179.3 0.1 multiply_reduce_fusion.3
  179.4 19.7 %all-reduce = (f32[32,256]{1,0:T(8,128)S(1)}, f32[32]{0:T(128)S(1)}) all-reduce(f32[32,256]{1,0:T(8,128)S(1)} %get-tuple-element.3, f32[32]{0:T(128)S(1)} %multiply_reduce_fusion.3), channel_id=1, replica_groups=mesh['walker'=4,'tangent'=4,'feat'=2] {'tangent'}, use_global_device_ids=true, to_apply=%region_11.0 | all-reduce | flops 8224 | bytes 65792 | tf_op jit(solution)/shard_map/psum | solution.py:56
  199.1 0.0 copy-done.2
  199.1 0.1 fusion.14
  199.2 3.0 %all-reduce.1 = (f32[32]{0:T(128)}, f32[32]{0:T(128)S(1)}) all-reduce(f32[32]{0:T(128)S(1)} %get-tuple-element.6, f32[32]{0:T(128)S(1)} %get-tuple-element.5), channel_id=1, replica_groups=mesh['walker'=4,'tangent'=4,'feat'=2] {'feat'}, use_global_device_ids=true, to_apply=%region_6.0 | all-reduce | flops 64 | bytes 512 | tf_op jit(solution)/shard_map/psum | solution.py:58
  202.2 0.5 add_multiply_fusion
  202.7 0.0 copy-done.3
  (1 shorter events, 0.0 us)
Async XLA Ops:
  7.2 50.4 %copy-start = (bf16[32,192,256]{2,1,0:T(8,128)(2,1)S(1)}, bf16[32,192,256]{2,1,0:T(8,128)(2,1)}, u32[]{:S(2)}) copy-start(bf16[32,192,256]{2,1,0:T(8,128)(2,1)} %param.9) | copy-start | bytes 9437188
  7.2 112.4 %reduce-scatter.5.cloned.1.call-start = ((), (), s32[]{:S(2)}) async-start(), calls=%async_computation.4 | async-start | bytes 196608 | tf_op jit(solution)/shard_map/reduce_scatter | solution.py:18
  57.5 63.0 %reduce-scatter.7.cloned.1.call-start = ((), (), s32[]{:S(2)}) async-start(), calls=%async_computation.5 | async-start | bytes 18874368 | tf_op jit(solution)/shard_map/reduce_scatter | solution.py:19
  77.4 0.7 copy-start.5
  77.4 0.8 copy-start.4
  77.4 75.5 %reduce-scatter.9.cloned.1.call-start = ((), (), s32[]{:S(2)}) async-start(), calls=%async_computation.6 | async-start | bytes 196608 | tf_op jit(solution)/shard_map/reduce_scatter | solution.py:18
  119.6 21.4 %copy-start.1 = (f32[2,32,256]{2,1,0:T(8,128)S(1)}, f32[2,32,256]{2,1,0:T(8,128)}, u32[]{:S(2)}) copy-start(f32[2,32,256]{2,1,0:T(8,128)} %reduce-scatter.5.cloned.1.call-done) | copy-start | bytes 196612
  142.8 29.0 %reduce-scatter.11.cloned.1.call-start = ((), (), s32[]{:S(2)}) async-start(), calls=%async_computation.7 | async-start | bytes 18874368 | tf_op jit(solution)/shard_map/reduce_scatter | solution.py:19
  152.1 0.7 copy-start.6
  152.1 0.8 copy-start.7
  152.9 46.2 %copy-start.2 = (f32[2,32,256]{2,1,0:T(8,128)S(1)}, f32[2,32,256]{2,1,0:T(8,128)}, u32[]{:S(2)}) copy-start(f32[2,32,256]{2,1,0:T(8,128)} %reduce-scatter.9.cloned.1.call-done) | copy-start | bytes 196612
  179.3 23.5 %copy-start.3 = (f32[32,192]{1,0:T(8,128)}, f32[32,192]{1,0:T(8,128)S(1)}, u32[]{:S(2)}) copy-start(f32[32,192]{1,0:T(8,128)S(1)} %psum.44) | copy-start | bytes 73732
Sparse Core Ops, SparseCore 0:
  57.6 3.7 reduce-scatter.4
  77.5 17.7 reduce-scatter.6
  142.9 4.0 reduce-scatter.8
  152.2 19.6 reduce-scatter.10
where the time goes:
time: 210 us; the launch traced here: 209 us
  blocking collectives  133 us (63%)
  matrix products  20.1 us (10%)
  waiting for transfers between devices  18.2 us (9%)
  local copies, waits for them, and re-layouts  14.1 us (7%)
  between operations  13.9 us (7%)
  other arithmetic  9.81 us (5%)
    all_gather x1, blocking collectives, per_device(): lax.all_gather(w_first, ('walker', 'tangent', 'feat'), axis=0, tiled=True)  48.4 us
    all_gather x1, blocking collectives, per_device(): lax.all_gather(w_second, ('walker', 'tangent', 'feat'), axis=0, tiled=True)  41.5 us
    psum x1, blocking collectives, per_device(): curv_second = lax.psum(local_squares, 'tangent')  19.7 us
    reduce_scatter x2, waiting for transfers between devices, tanh_layer(): lax.psum_scatter(partial_grad, 'feat', scatter_dimension=2, tiled=True)  18.1 us
    psum x1, blocking collectives, per_device(): curv_first = lax.psum(jnp.sum(grad_pre * grad_pre, axis=1), 'tangent')  17.1 us
    dot_general x2, matrix products, tanh_layer(): jnp.dot(tangents.reshape(count_w * count_t, half_width), w_rows, preferre...  16.5 us
    dot_general x1, local copies, waits for them, and re-layouts, tanh_layer(): jnp.dot(tangents.reshape(count_w * count_t, half_width), w_rows, preferre...  12.6 us
    psum x2, blocking collectives, per_device(): lax.psum((amp_part, grad_part, lap_part), 'feat')  6.39 us
  transfers between devices with their start and end apart: 4, of which 1 were waited for; matrix products, arithmetic and copies ran while one was open for 15% of the time, Pallas kernels for 0%

commit v1 on v0

v1 whole, which is shorter than its diff:
```python
import functools

import jax
import jax.numpy as jnp
from jax import lax
from jax.experimental import pallas as pl
from jax.experimental.pallas import tpu as pltpu
from jax.sharding import PartitionSpec as P

F32 = jnp.float32
BF16 = jnp.bfloat16
MESH = pl.DeviceIdType.MESH
CHUNK = 4


def dot(a, b):
    return jnp.dot(a, b, preferred_element_type=F32)


def dot_t(a, b):
    return lax.dot_general(a, b, (((1,), (1,)), ((), ())), preferred_element_type=F32)


def halves(a):
    high = a.astype(BF16)
    low = (a - high.astype(F32)).astype(BF16)
    return jnp.concatenate([high, low], axis=0)


def kernel(
    nw, nz, gather,
    value_ref, tang_ref, lap_ref, w1_ref, b1_ref, w2_ref, b2_ref, r_ref,
    grad_out, small_out,
    x, w1_all, w2_all, vl, vec, slope_s, curv1_s, curv2_s, gbuf, msg, small_s,
    loc, ps, pr, za_s, za_r, wb_s, wb_r, fc_s, fc_r, gs, gr, ms, mr,
):
    w, z, f = lax.axis_index("walker"), lax.axis_index("tangent"), lax.axis_index("feat")
    other = 1 - f
    own, cols, width = x.shape
    half = width // 2
    chunks = own // CHUNK
    mine = pl.ds(pl.multiple_of(f * own, own), own)
    theirs = pl.ds(pl.multiple_of(other * own, own), own)
    my_cols = pl.ds(pl.multiple_of(f * half, half), half)
    their_cols = pl.ds(pl.multiple_of(other * half, half), half)
    partner = (w, z, other)

    def z_at(k):
        return lax.rem(z + k, nz)

    def w_at(k):
        return lax.rem(w + k, nw)

    def remote(src, dst, send, recv, device):
        return pltpu.make_async_remote_copy(
            src_ref=src, dst_ref=dst, send_sem=send, recv_sem=recv, device_id=device, device_id_type=MESH
        )

    local = []

    def fetch(src, dst):
        copy = pltpu.make_async_copy(src, dst, loc.at[len(local)])
        copy.start()
        local.append(copy)
        return copy

    own_w = [
        fetch(src, dst.at[w, z, f] if gather else dst) for src, dst in ((w1_ref, w1_all), (w2_ref, w2_all))
    ]
    own_vec = [fetch(src, vec.at[i]) for i, src in enumerate((b1_ref, b2_ref, r_ref))]
    own_vl = [fetch(src.at[mine, :], vl.at[i, :, my_cols]) for i, src in enumerate((value_ref, lap_ref))]
    own_tang = []
    for c in range(chunks):
        rows = pl.ds(f * own + c * CHUNK, CHUNK)
        own_tang.append(fetch(tang_ref.at[rows], x.at[pl.ds(c * CHUNK, CHUNK), :, my_cols]))

    barrier = pltpu.get_barrier_semaphore()
    greeted = [partner]
    for k in range(1, nz):
        greeted += [(w, z_at(k), f), (w, z_at(k), other)]
    if gather:
        greeted += [(w_at(k), z, f) for k in range(1, nw)]
    for device in greeted:
        pl.semaphore_signal(barrier, inc=1, device_id=device, device_id_type=MESH)
    pl.semaphore_wait(barrier, len(greeted))

    sent = []

    def send(*args):
        copy = remote(*args)
        copy.start()
        sent.append(copy)

    def arrived(ref, send_sem, recv_sem):
        remote(ref, ref, send_sem, recv_sem, partner).wait_recv()

    weights = ((w1_ref, w1_all), (w2_ref, w2_all))

    def along_z(layer):
        src, dst = weights[layer]
        for k in range(1, nz):
            send(src, dst.at[w, z, f], za_s.at[layer, k], za_r.at[layer, k], (w, z_at(k), f))

    def to_partner(layer, k):
        dst = weights[layer][1]
        piece = dst.at[w_at(nw - k), :, f]
        send(piece, piece, fc_s.at[layer, k], fc_r.at[layer, k], partner)

    def across(layer):
        dst = weights[layer][1]
        own_w[layer].wait()
        for k in range(1, nz):
            arrived(dst.at[w, z_at(nz - k), f], za_s.at[layer, k], za_r.at[layer, k])
        piece = dst.at[w, :, f]
        for k in range(1, nw):
            send(piece, piece, wb_s.at[layer, k], wb_r.at[layer, k], (w_at(k), z, f))
        to_partner(layer, 0)

    def relay(layer):
        dst = weights[layer][1]
        for k in range(1, nw):
            arrived(dst.at[w_at(nw - k), :, f], wb_s.at[layer, k], wb_r.at[layer, k])
            to_partner(layer, k)

    def whole(layer):
        dst = weights[layer][1]
        if gather:
            for k in range(nw):
                arrived(dst.at[w_at(nw - k), :, other], fc_s.at[layer, k], fc_r.at[layer, k])
        else:
            own_w[layer].wait()
        return dst[...].reshape(width, width)

    if gather:
        along_z(0)
    for i, src in enumerate((value_ref, lap_ref)):
        send(src.at[theirs, :], vl.at[i, :, my_cols], ps.at[i], pr.at[i], partner)
    for c in range(chunks):
        rows = pl.ds(other * own + c * CHUNK, CHUNK)
        send(
            tang_ref.at[rows], x.at[pl.ds(c * CHUNK, CHUNK), :, my_cols],
            ps.at[2 + c], pr.at[2 + c], partner,
        )
    if gather:
        along_z(1)
        across(0)
        relay(0)
        across(1)

    for copy in own_vec + own_vl + own_tang:
        copy.wait()
    for i in range(2):
        arrived(vl.at[i, :, their_cols], ps.at[i], pr.at[i])
    for c in range(chunks):
        arrived(x.at[pl.ds(c * CHUNK, CHUNK), :, their_cols], ps.at[2 + c], pr.at[2 + c])
    b1, b2, readout = vec[0], vec[1], vec[2]

    w1 = whole(0)
    vl_one = dot(vl[...].reshape(2 * own, width), w1)
    hidden_one = jnp.tanh(vl_one[:own] + b1)
    lapin_one = vl_one[own:]
    slope_one = 1.0 - hidden_one * hidden_one
    bend_one = -2.0 * hidden_one * slope_one
    slope_s[...] = slope_one

    def first(c, carry):
        block = x[pl.ds(c * CHUNK, CHUNK)].reshape(CHUNK * cols, width)
        grad = dot(block, w1)
        for i in range(CHUNK):
            row = c * CHUNK + i
            g = grad[i * cols:(i + 1) * cols]
            curv1_s[pl.ds(row, 1), :] = jnp.sum(g * g, axis=0, keepdims=True)
            x[row] = (slope_s[pl.ds(row, 1), :] * g).astype(BF16)
        return carry

    lax.fori_loop(0, chunks, first, 0)

    if gather:
        relay(1)
    w2 = whole(1)
    hidden_two = jnp.tanh(dot(hidden_one.astype(BF16), w2) + b2)
    slope_two = 1.0 - hidden_two * hidden_two
    bend_two = -2.0 * hidden_two * slope_two
    back = dot_t(halves(readout * slope_two), w2)
    back = back[:own] + back[own:]
    back_terms = halves(back)
    term_row = lax.rem(lax.broadcasted_iota(jnp.int32, (2 * own, cols), 0), own)

    def second(c, carry):
        block = x[pl.ds(c * CHUNK, CHUNK)].reshape(CHUNK * cols, width)
        grad = dot(block, w2)
        for i in range(CHUNK):
            row = c * CHUNK + i
            g = grad[i * cols:(i + 1) * cols]
            curv2_s[pl.ds(row, 1), :] = jnp.sum(g * g, axis=0, keepdims=True)
            terms = dot_t(back_terms, x[row])
            gbuf[pl.ds(row, 1), :] = jnp.sum(jnp.where(term_row == row, terms, 0.0), axis=0, keepdims=True)
        return carry

    lax.fori_loop(0, chunks, second, 0)

    send(gbuf, grad_out.at[mine, :], gs, gr, partner)
    keep = pltpu.make_async_copy(gbuf, grad_out.at[mine, :], loc.at[len(local)])
    keep.start()
    gradient = gbuf[...]
    first_z = z == 0
    once = jnp.sum(back * slope_one * lapin_one, axis=1, keepdims=True)
    part = (
        jnp.sum(readout * bend_two * curv2_s[...] + back * bend_one * curv1_s[...], axis=1, keepdims=True)
        + jnp.sum(gradient * gradient, axis=1, keepdims=True)
        + jnp.where(first_z, once, 0.0)
    )
    amp = jnp.where(first_z, jnp.sum(readout * hidden_two, axis=1, keepdims=True), 0.0)
    lane = lax.broadcasted_iota(jnp.int32, (own, 128), 1)
    place = lane == lax.broadcasted_iota(jnp.int32, (own, 128), 0) + f * own
    kin_row = jnp.sum(jnp.where(place, part, 0.0), axis=0, keepdims=True)
    amp_row = jnp.sum(jnp.where(place, amp, 0.0), axis=0, keepdims=True)
    tile_row = lax.broadcasted_iota(jnp.int32, (8, 128), 0)
    msg[z, f] = jnp.where(tile_row == 0, amp_row, -0.5 * kin_row)
    slot = msg.at[z, f]
    others = [(k, g) for k in range(nz) for g in range(2) if k or g]
    for k, g in others:
        send(slot, slot, ms.at[k, g], mr.at[k, g], (w, z_at(k), other if g else f))
    for k, g in others:
        arrived(msg.at[z_at(nz - k), other if g else f], ms.at[k, g], mr.at[k, g])
    total = msg[0, 0] + msg[0, 1]
    for k in range(1, nz):
        total = total + (msg[k, 0] + msg[k, 1])
    small_s[...] = total
    last = pltpu.make_async_copy(small_s, small_out, loc.at[len(local) + 1])
    last.start()
    arrived(grad_out.at[theirs, :], gs, gr)
    keep.wait()
    last.wait()
    for copy in sent:
        copy.wait_send()


def per_device(nw, nz, value_in, tang_in, lap_in, w_first, b_first, w_second, b_second, readout):
    walkers, cols, half = tang_in.shape
    width, own = 2 * half, walkers // 2
    shard = w_first.shape[0]
    gather = shard % 16 == 0
    if gather:
        w_shape = (nw, nz, 2, shard, width)
    else:
        w_shape = (width, width)
        w_first, w_second = (
            lax.all_gather(a, ("walker", "tangent", "feat"), axis=0, tiled=True) for a in (w_first, w_second)
        )
    chunks = own // CHUNK
    dma = pltpu.SemaphoreType.DMA
    anywhere = pl.BlockSpec(memory_space=pl.ANY)
    rows = own * cols
    grad, small = pl.pallas_call(
        functools.partial(kernel, nw, nz, gather),
        out_shape=(
            jax.ShapeDtypeStruct((walkers, cols), F32),
            jax.ShapeDtypeStruct((8, 128), F32),
        ),
        in_specs=[anywhere] * 8,
        out_specs=(anywhere, anywhere),
        scratch_shapes=[
            pltpu.VMEM((own, cols, width), BF16),
            pltpu.VMEM(w_shape, BF16),
            pltpu.VMEM(w_shape, BF16),
            pltpu.VMEM((2, own, width), BF16),
            pltpu.VMEM((3, 1, width), F32),
            pltpu.VMEM((own, width), F32),
            pltpu.VMEM((own, width), F32),
            pltpu.VMEM((own, width), F32),
            pltpu.VMEM((own, cols), F32),
            pltpu.VMEM((nz, 2, 8, 128), F32),
            pltpu.VMEM((8, 128), F32),
            dma((9 + chunks,)),
            dma((2 + chunks,)),
            dma((2 + chunks,)),
            dma((2, nz)),
            dma((2, nz)),
            dma((2, nw)),
            dma((2, nw)),
            dma((2, nw)),
            dma((2, nw)),
            dma,
            dma,
            dma((nz, 2)),
            dma((nz, 2)),
        ],
        compiler_params=pltpu.CompilerParams(
            collective_id=0, has_side_effects=True, vmem_limit_bytes=50 * 2**20
        ),
        cost_estimate=pl.CostEstimate(
            flops=4 * rows * width * width, bytes_accessed=2 * rows * width, transcendentals=0
        ),
    )(
        value_in, tang_in, lap_in, w_first, b_first.reshape(1, width),
        w_second, b_second.reshape(1, width), readout.reshape(1, width),
    )
    return (small[0, :walkers], grad, small[1, :walkers])


def solution(mesh):
    placed = (
        P("walker", "feat"),
        P("walker", "tangent", "feat"),
        P("walker", "feat"),
        P(("walker", "tangent", "feat"), None),
        P(),
        P(("walker", "tangent", "feat"), None),
        P(),
        P(),
    )
    return jax.shard_map(
        functools.partial(per_device, mesh.shape["walker"], mesh.shape["tangent"]),
        mesh=mesh,
        in_specs=placed,
        out_specs=(P("walker"), P("walker", "tangent"), P("walker")),
        check_vma=False,
    )
```

time: 210 us -> 36.5 us (0.17)
  blocking collectives: 133 us -> 0 us
  Pallas kernels: 0 us -> 27.3 us
  matrix products: 20.1 us -> 0 us
  waiting for transfers between devices: 18.2 us -> 0 us
  between operations: 13.9 us -> 0.66 us
  other arithmetic: 9.81 us -> 0 us
  local copies, waits for them, and re-layouts: 14.1 us -> 7.93 us
    all_gather x2 -> x0, blocking collectives: 89.9 us -> none  [the longest x1 48.4 us: per_device(): lax.all_gather(w_first, ('walker', 'tangent', 'feat'), axis=0, tiled=True)]
    psum x4 -> x0, blocking collectives: 43.2 us -> none  [the longest x1 19.7 us: per_device(): curv_second = lax.psum(local_squares, 'tangent')]
    pallas_call x0 -> x1, Pallas kernels: none -> 27.3 us  [per_device(): pl.pallas_call(functools.partial(kernel, nw, nz, gather), out_shape=(jax....]
    dot_general x4 -> x0, matrix products: 20.1 us -> none  [the longest x2 16.5 us: tanh_layer(): jnp.dot(tangents.reshape(count_w * count_t, half_width), w_rows, preferre...]
    reduce_scatter x4 -> x0, waiting for transfers between devices: 18.1 us -> none  [the longest x2 18.1 us: tanh_layer(): lax.psum_scatter(partial_grad, 'feat', scatter_dimension=2, tiled=True)]
    dot_general x1 -> x0, local copies, waits for them, and re-layouts: 12.6 us -> none  [tanh_layer(): jnp.dot(tangents.reshape(count_w * count_t, half_width), w_rows, preferre...]
    reduce_sum x4 -> x0, other arithmetic: 7.58 us -> none  [the longest x1 3.97 us: per_device(): local_squares = jnp.sum(grad_pre * grad_pre, axis=1)]
    unnamed x16 -> x17, local copies, waits for them, and re-layouts: 1.29 us -> 7.41 us
  transfers between devices with their start and end apart: 4 -> 0, of which waited for: 1 -> 0; matrix products, arithmetic and copies ran while one was open for 15% -> 0% of each run, Pallas kernels for 0% -> 0%
where the time goes in v1:
time: 36.5 us; the launch traced here: 35.9 us
  Pallas kernels  27.3 us (75%)
  local copies, waits for them, and re-layouts  7.93 us (22%)
  between operations  0.66 us (2%)
    pallas_call x1, Pallas kernels, per_device(): pl.pallas_call(functools.partial(kernel, nw, nz, gather), out_shape=(jax....  27.3 us
    unnamed x17, local copies, waits for them, and re-layouts  7.41 us

profile of v1, /device:TPU:0, one launch (start us, length us, event | category | flops | bytes accessed | tf_op | source)
XLA Modules:
  0.0 35.9 jit_solution(11867654917989897388)
XLA Ops:
  0.6 0.0 copy-start
  0.6 1.9 %copy-done = bf16[32,192,256]{2,1,0:T(8,128)(2,1)S(1)} copy-done((bf16[32,192,256]{2,1,0:T(8,128)(2,1)S(1)}, bf16[32,192,256]{2,1,0:T(8,128)(2,1)}, u32[]{:S(2)}) %copy-start) | copy-done | bytes 3145752
  2.5 0.0 copy-start.1
  2.5 0.7 %copy-done.1 = bf16[32,256]{1,0:T(8,128)(2,1)S(1)} copy-done((bf16[32,256]{1,0:T(8,128)(2,1)S(1)}, bf16[32,256]{1,0:T(8,128)(2,1)}, u32[]{:S(2)}) %copy-start.1) | copy-done | bytes 16408
  3.2 0.0 copy-start.2
  3.2 0.7 %copy-done.2 = bf16[32,256]{1,0:T(8,128)(2,1)S(1)} copy-done((bf16[32,256]{1,0:T(8,128)(2,1)S(1)}, bf16[32,256]{1,0:T(8,128)(2,1)}, u32[]{:S(2)}) %copy-start.2) | copy-done | bytes 16408
  4.0 0.0 copy-start.3
  4.0 0.7 %copy-done.3 = bf16[16,512]{1,0:T(8,128)(2,1)S(1)} copy-done((bf16[16,512]{1,0:T(8,128)(2,1)S(1)}, bf16[16,512]{1,0:T(8,128)(2,1)}, u32[]{:S(2)}) %copy-start.3) | copy-done | bytes 16408
  4.7 0.0 copy-start.4
  4.7 0.7 %copy-done.4 = bf16[16,512]{1,0:T(8,128)(2,1)S(1)} copy-done((bf16[16,512]{1,0:T(8,128)(2,1)S(1)}, bf16[16,512]{1,0:T(8,128)(2,1)}, u32[]{:S(2)}) %copy-start.4) | copy-done | bytes 16408
  5.4 0.0 copy-start.5
  5.4 0.7 %copy-done.5 = f32[512]{0:T(512)S(1)} copy-done((f32[512]{0:T(512)S(1)}, f32[512]{0:T(512)}, u32[]{:S(2)}) %copy-start.5) | copy-done | bytes 2072
  6.1 0.0 copy-start.6
  6.1 0.7 %copy-done.6 = f32[512]{0:T(512)S(1)} copy-done((f32[512]{0:T(512)S(1)}, f32[512]{0:T(512)}, u32[]{:S(2)}) %copy-start.6) | copy-done | bytes 2072
  6.8 0.0 copy-start.7
  6.8 0.7 %copy-done.7 = f32[512]{0:T(512)S(1)} copy-done((f32[512]{0:T(512)S(1)}, f32[512]{0:T(512)}, u32[]{:S(2)}) %copy-start.7) | copy-done | bytes 2072
  7.4 27.3 %shard_map.103 = (f32[32,192]{1,0:T(8,128)S(1)}, f32[8,128]{1,0:T(8,128)S(1)}) custom-call(bf16[32,256]{1,0:T(8,128)(2,1)S(1)} %copy-done.1, bf16[32,192,256]{2,1,0:T(8,128)(2,1)S(1)} %copy-done, bf16[32,256]{1,0:T(8,128)(2,1)S(1)} %copy-done.2, bf16[16,512]{1,0:T(8,128)(2,1)S(1)} %copy-done.3, f32[1,512]{1,0:T(1,128)S(1)} %bitcast.7, ...), custom_call_target="tpu_custom_call" | custom-call | flops 3221225472 | bytes 3145728 | tf_op jit(solution)/shard_map/pallas_call | solution.py:255
  34.7 0.5 %slice_bitcast_fusion = (f32[32]{0:T(128)}, f32[32]{0:T(128)}) fusion(f32[8,128]{1,0:T(8,128)S(1)} %get-tuple-element.5), kind=kLoop, calls=%fused_computation | loop fusion | bytes 512 | tf_op jit(solution)/shard_map/squeeze | solution.py:299
  35.3 0.6 %copy.12 = f32[32,192]{1,0:T(8,128)} copy(f32[32,192]{1,0:T(8,128)S(1)} %get-tuple-element.13) | data formatting | bytes 49152
Async XLA Ops:
  0.6 1.9 %copy-start = (bf16[32,192,256]{2,1,0:T(8,128)(2,1)S(1)}, bf16[32,192,256]{2,1,0:T(8,128)(2,1)}, u32[]{:S(2)}) copy-start(bf16[32,192,256]{2,1,0:T(8,128)(2,1)} %tang_ref.1) | copy-start | bytes 9437188
  2.5 0.7 %copy-start.1 = (bf16[32,256]{1,0:T(8,128)(2,1)S(1)}, bf16[32,256]{1,0:T(8,128)(2,1)}, u32[]{:S(2)}) copy-start(bf16[32,256]{1,0:T(8,128)(2,1)} %value_ref.1) | copy-start | bytes 49156
  3.2 0.7 %copy-start.2 = (bf16[32,256]{1,0:T(8,128)(2,1)S(1)}, bf16[32,256]{1,0:T(8,128)(2,1)}, u32[]{:S(2)}) copy-start(bf16[32,256]{1,0:T(8,128)(2,1)} %lap_ref.1) | copy-start | bytes 49156
  4.0 0.7 %copy-start.3 = (bf16[16,512]{1,0:T(8,128)(2,1)S(1)}, bf16[16,512]{1,0:T(8,128)(2,1)}, u32[]{:S(2)}) copy-start(bf16[16,512]{1,0:T(8,128)(2,1)} %w1_ref.1) | copy-start | bytes 49156
  4.7 0.7 %copy-start.4 = (bf16[16,512]{1,0:T(8,128)(2,1)S(1)}, bf16[16,512]{1,0:T(8,128)(2,1)}, u32[]{:S(2)}) copy-start(bf16[16,512]{1,0:T(8,128)(2,1)} %w2_ref.1) | copy-start | bytes 49156
  5.4 0.7 %copy-start.5 = (f32[512]{0:T(512)S(1)}, f32[512]{0:T(512)}, u32[]{:S(2)}) copy-start(f32[512]{0:T(512)} %param.12) | copy-start | bytes 6148
  6.1 0.7 %copy-start.6 = (f32[512]{0:T(512)S(1)}, f32[512]{0:T(512)}, u32[]{:S(2)}) copy-start(f32[512]{0:T(512)} %param.14) | copy-start | bytes 6148
  6.8 0.7 %copy-start.7 = (f32[512]{0:T(512)S(1)}, f32[512]{0:T(512)}, u32[]{:S(2)}) copy-start(f32[512]{0:T(512)} %param.15) | copy-start | bytes 6148

commit v2 on v1

--- a/solution.py
+++ b/solution.py
@@ -17,10 +17,6 @@
     return jnp.dot(a, b, preferred_element_type=F32)
 
 
-def dot_t(a, b):
-    return lax.dot_general(a, b, (((1,), (1,)), ((), ())), preferred_element_type=F32)
-
-
 def halves(a):
     high = a.astype(BF16)
     low = (a - high.astype(F32)).astype(BF16)
@@ -30,8 +26,8 @@
 def kernel(
     nw, nz, gather,
     value_ref, tang_ref, lap_ref, w1_ref, b1_ref, w2_ref, b2_ref, r_ref,
-    grad_out, small_out,
-    x, w1_all, w2_all, vl, vec, slope_s, curv1_s, curv2_s, gbuf, msg, small_s,
+    out,
+    x, w1_all, w2_all, vl, vec, slope_s, weight_s, curv1_s, curv2_s, msg,
     loc, ps, pr, za_s, za_r, wb_s, wb_r, fc_s, fc_r, gs, gr, ms, mr,
 ):
     w, z, f = lax.axis_index("walker"), lax.axis_index("tangent"), lax.axis_index("feat")
@@ -101,38 +97,35 @@
         for k in range(1, nz):
             send(src, dst.at[w, z, f], za_s.at[layer, k], za_r.at[layer, k], (w, z_at(k), f))
 
-    def to_partner(layer, k):
+    def pass_across(layer, k):
+        src, dst = weights[layer]
+        piece = dst.at[w, z_at(nz - k), f]
+        if k:
+            arrived(piece, za_s.at[layer, k], za_r.at[layer, k])
+        for j in range(1, nw):
+            send(src if k == 0 else piece, piece, wb_s.at[layer, k, j], wb_r.at[layer, k, j], (w_at(j), z, f))
+
+    def pass_over(layer, k):
         dst = weights[layer][1]
-        piece = dst.at[w_at(nw - k), :, f]
+        if k == 0:
+            own_w[layer].wait()
+        for j in range(1, nw):
+            arrived(dst.at[w_at(nw - j), z_at(nz - k), f], wb_s.at[layer, k, j], wb_r.at[layer, k, j])
+        piece = dst.at[:, z_at(nz - k), f]
         send(piece, piece, fc_s.at[layer, k], fc_r.at[layer, k], partner)
-
-    def across(layer):
-        dst = weights[layer][1]
-        own_w[layer].wait()
-        for k in range(1, nz):
-            arrived(dst.at[w, z_at(nz - k), f], za_s.at[layer, k], za_r.at[layer, k])
-        piece = dst.at[w, :, f]
-        for k in range(1, nw):
-            send(piece, piece, wb_s.at[layer, k], wb_r.at[layer, k], (w_at(k), z, f))
-        to_partner(layer, 0)
-
-    def relay(layer):
-        dst = weights[layer][1]
-        for k in range(1, nw):
-            arrived(dst.at[w_at(nw - k), :, f], wb_s.at[layer, k], wb_r.at[layer, k])
-            to_partner(layer, k)
 
     def whole(layer):
         dst = weights[layer][1]
         if gather:
-            for k in range(nw):
-                arrived(dst.at[w_at(nw - k), :, other], fc_s.at[layer, k], fc_r.at[layer, k])
+            for k in range(nz):
+                arrived(dst.at[:, z_at(nz - k), other], fc_s.at[layer, k], fc_r.at[layer, k])
         else:
             own_w[layer].wait()
         return dst[...].reshape(width, width)
 
     if gather:
         along_z(0)
+        pass_across(0, 0)
     for i, src in enumerate((value_ref, lap_ref)):
         send(src.at[theirs, :], vl.at[i, :, my_cols], ps.at[i], pr.at[i], partner)
     for c in range(chunks):
@@ -143,9 +136,12 @@
         )
     if gather:
         along_z(1)
-        across(0)
-        relay(0)
-        across(1)
+        for k in range(1, nz):
+            pass_across(0, k)
+            pass_over(0, k - 1)
+        pass_over(0, nz - 1)
+        for k in range(nz):
+            pass_across(1, k)
 
     for copy in own_vec + own_vl + own_tang:
         copy.wait()
@@ -173,18 +169,21 @@
             x[row] = (slope_s[pl.ds(row, 1), :] * g).astype(BF16)
         return carry
 
-    lax.fori_loop(0, chunks, first, 0)
-
-    if gather:
-        relay(1)
+    lax.fori_loop(0, chunks - 1, first, 0)
+    if gather:
+        for k in range(nz):
+            pass_over(1, k)
+    first(chunks - 1, 0)
+
     w2 = whole(1)
-    hidden_two = jnp.tanh(dot(hidden_one.astype(BF16), w2) + b2)
+    first_z = z == 0
+    lap_two = bend_one * curv1_s[...] + jnp.where(first_z, slope_one * lapin_one, 0.0)
+    vl_two = dot(jnp.concatenate([hidden_one.astype(BF16), halves(lap_two)], axis=0), w2)
+    hidden_two = jnp.tanh(vl_two[:own] + b2)
+    lapin_two = vl_two[own:2 * own] + vl_two[2 * own:]
     slope_two = 1.0 - hidden_two * hidden_two
     bend_two = -2.0 * hidden_two * slope_two
-    back = dot_t(halves(readout * slope_two), w2)
-    back = back[:own] + back[own:]
-    back_terms = halves(back)
-    term_row = lax.rem(lax.broadcasted_iota(jnp.int32, (2 * own, cols), 0), own)
+    weight_s[...] = readout * slope_two
 
     def second(c, carry):
         block = x[pl.ds(c * CHUNK, CHUNK)].reshape(CHUNK * cols, width)
@@ -193,23 +192,18 @@
             row = c * CHUNK + i
             g = grad[i * cols:(i + 1) * cols]
             curv2_s[pl.ds(row, 1), :] = jnp.sum(g * g, axis=0, keepdims=True)
-            terms = dot_t(back_terms, x[row])
-            gbuf[pl.ds(row, 1), :] = jnp.sum(jnp.where(term_row == row, terms, 0.0), axis=0, keepdims=True)
+            terms = weight_s[pl.ds(row, 1), :] * g
+            terms = sum(terms[:, j:j + 128] for j in range(0, width, 128))
+            out[pl.ds(f * own + row, 1), 0:cols] = jnp.sum(terms.T, axis=0, keepdims=True)
         return carry
 
     lax.fori_loop(0, chunks, second, 0)
 
-    send(gbuf, grad_out.at[mine, :], gs, gr, partner)
-    keep = pltpu.make_async_copy(gbuf, grad_out.at[mine, :], loc.at[len(local)])
-    keep.start()
-    gradient = gbuf[...]
-    first_z = z == 0
-    once = jnp.sum(back * slope_one * lapin_one, axis=1, keepdims=True)
-    part = (
-        jnp.sum(readout * bend_two * curv2_s[...] + back * bend_one * curv1_s[...], axis=1, keepdims=True)
-        + jnp.sum(gradient * gradient, axis=1, keepdims=True)
-        + jnp.where(first_z, once, 0.0)
-    )
+    send(out.at[mine, :], out.at[mine, :], gs, gr, partner)
+    gradient = out[mine, 0:cols]
+    part = jnp.sum(
+        readout * (slope_two * lapin_two + bend_two * curv2_s[...]), axis=1, keepdims=True
+    ) + jnp.sum(gradient * gradient, axis=1, keepdims=True)
     amp = jnp.where(first_z, jnp.sum(readout * hidden_two, axis=1, keepdims=True), 0.0)
     lane = lax.broadcasted_iota(jnp.int32, (own, 128), 1)
     place = lane == lax.broadcasted_iota(jnp.int32, (own, 128), 0) + f * own
@@ -226,12 +220,8 @@
     total = msg[0, 0] + msg[0, 1]
     for k in range(1, nz):
         total = total + (msg[k, 0] + msg[k, 1])
-    small_s[...] = total
-    last = pltpu.make_async_copy(small_s, small_out, loc.at[len(local) + 1])
-    last.start()
-    arrived(grad_out.at[theirs, :], gs, gr)
-    keep.wait()
-    last.wait()
+    out[2 * own:2 * own + 8, 0:128] = total
+    arrived(out.at[theirs, :], gs, gr)
     for copy in sent:
         copy.wait_send()
 
@@ -250,16 +240,13 @@
         )
     chunks = own // CHUNK
     dma = pltpu.SemaphoreType.DMA
-    anywhere = pl.BlockSpec(memory_space=pl.ANY)
+    in_hbm = pl.BlockSpec(memory_space=pltpu.HBM)
     rows = own * cols
-    grad, small = pl.pallas_call(
+    out = pl.pallas_call(
         functools.partial(kernel, nw, nz, gather),
-        out_shape=(
-            jax.ShapeDtypeStruct((walkers, cols), F32),
-            jax.ShapeDtypeStruct((8, 128), F32),
-        ),
-        in_specs=[anywhere] * 8,
-        out_specs=(anywhere, anywhere),
+        out_shape=jax.ShapeDtypeStruct((walkers + 8, cols if cols > 128 else 128), F32),
+        in_specs=[in_hbm] * 8,
+        out_specs=pl.BlockSpec(memory_space=pltpu.VMEM),
         scratch_shapes=[
             pltpu.VMEM((own, cols, width), BF16),
             pltpu.VMEM(w_shape, BF16),
@@ -269,25 +256,24 @@
             pltpu.VMEM((own, width), F32),
             pltpu.VMEM((own, width), F32),
             pltpu.VMEM((own, width), F32),
-            pltpu.VMEM((own, cols), F32),
+            pltpu.VMEM((own, width), F32),
             pltpu.VMEM((nz, 2, 8, 128), F32),
-            pltpu.VMEM((8, 128), F32),
-            dma((9 + chunks,)),
+            dma((7 + chunks,)),
             dma((2 + chunks,)),
             dma((2 + chunks,)),
             dma((2, nz)),
             dma((2, nz)),
-            dma((2, nw)),
-            dma((2, nw)),
-            dma((2, nw)),
-            dma((2, nw)),
+            dma((2, nz, nw)),
+            dma((2, nz, nw)),
+            dma((2, nz)),
+            dma((2, nz)),
             dma,
             dma,
             dma((nz, 2)),
             dma((nz, 2)),
         ],
         compiler_params=pltpu.CompilerParams(
-            collective_id=0, has_side_effects=True, vmem_limit_bytes=50 * 2**20
+            collective_id=0, has_side_effects=True, vmem_limit_bytes=64 * 2**20
         ),
         cost_estimate=pl.CostEstimate(
             flops=4 * rows * width * width, bytes_accessed=2 * rows * width, transcendentals=0
@@ -296,7 +282,7 @@
         value_in, tang_in, lap_in, w_first, b_first.reshape(1, width),
         w_second, b_second.reshape(1, width), readout.reshape(1, width),
     )
-    return (small[0, :walkers], grad, small[1, :walkers])
+    return (out[walkers, :walkers], out[:walkers, :cols], out[walkers + 1, :walkers])
 
 
 def solution(mesh):

time: 36.5 us -> 32.2 us (0.88); the launches traced: 35.9 us -> 32 us
  local copies, waits for them, and re-layouts: 7.93 us -> 2.65 us
  Pallas kernels: 27.3 us -> 28.7 us
    unnamed x17 -> x0, local copies, waits for them, and re-layouts: 7.41 us -> none
    pallas_call x1, Pallas kernels: 27.3 us -> 28.7 us  [per_device(): pl.pallas_call(functools.partial(kernel, nw, nz, gather), out_shape=jax.S...]
    slice x0 -> x1, local copies, waits for them, and re-layouts: none -> 1.37 us  [per_device(): out[:walkers, :cols]]
    squeeze x1, local copies, waits for them, and re-layouts: 0.52 us -> 1.27 us  [per_device(): out[walkers + 1, :walkers]]
where the time goes in v2:
time: 32.2 us; the launch traced here: 32 us
  Pallas kernels  28.7 us (89%)
  local copies, waits for them, and re-layouts  2.65 us (8%)
  between operations  0.64 us (2%)
    pallas_call x1, Pallas kernels, per_device(): pl.pallas_call(functools.partial(kernel, nw, nz, gather), out_shape=jax.S...  28.7 us
    slice x1, local copies, waits for them, and re-layouts, per_device(): out[:walkers, :cols]  1.37 us
    squeeze x1, local copies, waits for them, and re-layouts, per_device(): out[walkers + 1, :walkers]  1.27 us

profile of v2, /device:TPU:0, one launch (start us, length us, event | category | flops | bytes accessed | tf_op | source)
XLA Modules:
  0.0 32.0 jit_solution(807413539622099114)
XLA Ops:
  0.6 28.7 %shard_map.103 = f32[40,192]{1,0:T(8,128)} custom-call(bf16[32,256]{1,0:T(8,128)(2,1)} %value_ref.1, bf16[32,192,256]{2,1,0:T(8,128)(2,1)} %tang_ref.1, bf16[32,256]{1,0:T(8,128)(2,1)} %lap_ref.1, bf16[16,512]{1,0:T(8,128)(2,1)} %w1_ref.1, f32[1,512]{1,0:T(1,128)} %bitcast.7, bf16[16,512]{1,0:T(8,128)(2,1)} %w2_ref.1, f32[1,512]{1,0:T(1,128)} %bitcast.8, ...), custom_call_target="tpu_custom_call" | custom-call | flops 3221225472 | bytes 3145728 | tf_op jit(solution)/shard_map/pallas_call | solution.py:245
  29.3 1.3 %slice_bitcast_fusion = (f32[32]{0:T(128)}, f32[32]{0:T(128)}) fusion(f32[40,192]{1,0:T(8,128)} %shard_map.103), kind=kLoop, calls=%fused_computation | loop fusion | bytes 512 | tf_op jit(solution)/shard_map/squeeze | solution.py:285
  30.6 1.4 %slice.10 = f32[32,192]{1,0:T(8,128)} slice(f32[40,192]{1,0:T(8,128)} %shard_map.103), slice={[0:32], [0:192]} | slice | bytes 49152 | tf_op jit(solution)/shard_map/slice | solution.py:285

commit v3 on v2

--- a/solution.py
+++ b/solution.py
@@ -26,9 +26,9 @@
 def kernel(
     nw, nz, gather,
     value_ref, tang_ref, lap_ref, w1_ref, b1_ref, w2_ref, b2_ref, r_ref,
-    out,
-    x, w1_all, w2_all, vl, vec, slope_s, weight_s, curv1_s, curv2_s, msg,
-    loc, ps, pr, za_s, za_r, wb_s, wb_r, fc_s, fc_r, gs, gr, ms, mr,
+    grad_out, amp_out, kin_out,
+    x, w1_all, w2_all, vl, vec, slope_s, weight_s, curv1_s, curv2_s, gbuf, msg,
+    loc, ps, pr, za_s, za_r, wb_s, wb_r, fc_s, fc_r, vb_s, vb_r, vc_s, vc_r, gs, gr, ms, mr,
 ):
     w, z, f = lax.axis_index("walker"), lax.axis_index("tangent"), lax.axis_index("feat")
     other = 1 - f
@@ -65,10 +65,10 @@
     ]
     own_vec = [fetch(src, vec.at[i]) for i, src in enumerate((b1_ref, b2_ref, r_ref))]
     own_vl = [fetch(src.at[mine, :], vl.at[i, :, my_cols]) for i, src in enumerate((value_ref, lap_ref))]
-    own_tang = []
+    tang_at = len(local)
     for c in range(chunks):
         rows = pl.ds(f * own + c * CHUNK, CHUNK)
-        own_tang.append(fetch(tang_ref.at[rows], x.at[pl.ds(c * CHUNK, CHUNK), :, my_cols]))
+        fetch(tang_ref.at[rows], x.at[pl.ds(c * CHUNK, CHUNK), :, my_cols])
 
     barrier = pltpu.get_barrier_semaphore()
     greeted = [partner]
@@ -78,6 +78,9 @@
         greeted += [(w_at(k), z, f) for k in range(1, nw)]
     for device in greeted:
         pl.semaphore_signal(barrier, inc=1, device_id=device, device_id_type=MESH)
+    if gather:
+        for copy in own_w:
+            copy.wait()
     pl.semaphore_wait(barrier, len(greeted))
 
     sent = []
@@ -90,65 +93,86 @@
     def arrived(ref, send_sem, recv_sem):
         remote(ref, ref, send_sem, recv_sem, partner).wait_recv()
 
-    weights = ((w1_ref, w1_all), (w2_ref, w2_all))
+    weights = (w1_all, w2_all)
 
     def along_z(layer):
-        src, dst = weights[layer]
+        piece = weights[layer].at[w, z, f]
         for k in range(1, nz):
-            send(src, dst.at[w, z, f], za_s.at[layer, k], za_r.at[layer, k], (w, z_at(k), f))
-
-    def pass_across(layer, k):
-        src, dst = weights[layer]
-        piece = dst.at[w, z_at(nz - k), f]
-        if k:
-            arrived(piece, za_s.at[layer, k], za_r.at[layer, k])
+            send(piece, piece, za_s.at[layer, k], za_r.at[layer, k], (w, z_at(k), f))
+
+    def from_z(layer, k):
+        arrived(weights[layer].at[w, z_at(nz - k), f], za_s.at[layer, k], za_r.at[layer, k])
+
+    def pass_across(k):
+        piece = w1_all.at[w, z_at(nz - k), f]
         for j in range(1, nw):
-            send(src if k == 0 else piece, piece, wb_s.at[layer, k, j], wb_r.at[layer, k, j], (w_at(j), z, f))
-
-    def pass_over(layer, k):
-        dst = weights[layer][1]
-        if k == 0:
+            send(piece, piece, wb_s.at[k, j], wb_r.at[k, j], (w_at(j), z, f))
+
+    def pass_over(k):
+        for j in range(1, nw):
+            arrived(w1_all.at[w_at(nw - j), z_at(nz - k), f], wb_s.at[k, j], wb_r.at[k, j])
+        piece = w1_all.at[:, z_at(nz - k), f]
+        send(piece, piece, fc_s.at[k], fc_r.at[k], partner)
+
+    def second_across():
+        piece = w2_all.at[w, :, f]
+        for j in range(1, nw):
+            send(piece, piece, vb_s.at[j], vb_r.at[j], (w_at(j), z, f))
+
+    def second_over(j):
+        piece = w2_all.at[w_at(nw - j), :, f]
+        if j:
+            arrived(piece, vb_s.at[j], vb_r.at[j])
+        send(piece, piece, vc_s.at[j], vc_r.at[j], partner)
+
+    def whole(layer):
+        dst = weights[layer]
+        if not gather:
             own_w[layer].wait()
-        for j in range(1, nw):
-            arrived(dst.at[w_at(nw - j), z_at(nz - k), f], wb_s.at[layer, k, j], wb_r.at[layer, k, j])
-        piece = dst.at[:, z_at(nz - k), f]
-        send(piece, piece, fc_s.at[layer, k], fc_r.at[layer, k], partner)
-
-    def whole(layer):
-        dst = weights[layer][1]
-        if gather:
+        elif layer == 0:
             for k in range(nz):
-                arrived(dst.at[:, z_at(nz - k), other], fc_s.at[layer, k], fc_r.at[layer, k])
+                arrived(dst.at[:, z_at(nz - k), other], fc_s.at[k], fc_r.at[k])
         else:
-            own_w[layer].wait()
+            for j in range(nw):
+                arrived(dst.at[w_at(nw - j), :, other], vc_s.at[j], vc_r.at[j])
         return dst[...].reshape(width, width)
 
-    if gather:
-        along_z(0)
-        pass_across(0, 0)
-    for i, src in enumerate((value_ref, lap_ref)):
-        send(src.at[theirs, :], vl.at[i, :, my_cols], ps.at[i], pr.at[i], partner)
-    for c in range(chunks):
+    def give(c):
         rows = pl.ds(other * own + c * CHUNK, CHUNK)
         send(
             tang_ref.at[rows], x.at[pl.ds(c * CHUNK, CHUNK), :, my_cols],
             ps.at[2 + c], pr.at[2 + c], partner,
         )
+
+    if gather:
+        along_z(0)
+        pass_across(0)
+    for i, src in enumerate((value_ref, lap_ref)):
+        send(src.at[theirs, :], vl.at[i, :, my_cols], ps.at[i], pr.at[i], partner)
+    give(0)
     if gather:
         along_z(1)
         for k in range(1, nz):
-            pass_across(0, k)
-            pass_over(0, k - 1)
-        pass_over(0, nz - 1)
-        for k in range(nz):
-            pass_across(1, k)
-
-    for copy in own_vec + own_vl + own_tang:
+            from_z(0, k)
+            pass_across(k)
+            if k < chunks:
+                give(k)
+            pass_over(k - 1)
+        pass_over(nz - 1)
+        for c in range(nz, chunks):
+            give(c)
+        for k in range(1, nz):
+            from_z(1, k)
+        second_across()
+        second_over(0)
+    else:
+        for c in range(1, chunks):
+            give(c)
+
+    for copy in own_vec + own_vl:
         copy.wait()
     for i in range(2):
         arrived(vl.at[i, :, their_cols], ps.at[i], pr.at[i])
-    for c in range(chunks):
-        arrived(x.at[pl.ds(c * CHUNK, CHUNK), :, their_cols], ps.at[2 + c], pr.at[2 + c])
     b1, b2, readout = vec[0], vec[1], vec[2]
 
     w1 = whole(0)
@@ -160,6 +184,9 @@
     slope_s[...] = slope_one
 
     def first(c, carry):
+        own_part = x.at[pl.ds(c * CHUNK, CHUNK), :, my_cols]
+        pltpu.make_async_copy(own_part, own_part, loc.at[tang_at + c]).wait()
+        arrived(x.at[pl.ds(c * CHUNK, CHUNK), :, their_cols], ps.at[2 + c], pr.at[2 + c])
         block = x[pl.ds(c * CHUNK, CHUNK)].reshape(CHUNK * cols, width)
         grad = dot(block, w1)
         for i in range(CHUNK):
@@ -171,8 +198,8 @@
 
     lax.fori_loop(0, chunks - 1, first, 0)
     if gather:
-        for k in range(nz):
-            pass_over(1, k)
+        for j in range(1, nw):
+            second_over(j)
     first(chunks - 1, 0)
 
     w2 = whole(1)
@@ -194,13 +221,15 @@
             curv2_s[pl.ds(row, 1), :] = jnp.sum(g * g, axis=0, keepdims=True)
             terms = weight_s[pl.ds(row, 1), :] * g
             terms = sum(terms[:, j:j + 128] for j in range(0, width, 128))
-            out[pl.ds(f * own + row, 1), 0:cols] = jnp.sum(terms.T, axis=0, keepdims=True)
+            gbuf[pl.ds(row, 1), :] = jnp.sum(terms.T, axis=0, keepdims=True)
         return carry
 
     lax.fori_loop(0, chunks, second, 0)
 
-    send(out.at[mine, :], out.at[mine, :], gs, gr, partner)
-    gradient = out[mine, 0:cols]
+    send(gbuf, grad_out.at[mine, :], gs, gr, partner)
+    keep = pltpu.make_async_copy(gbuf, grad_out.at[mine, :], loc.at[len(local)])
+    keep.start()
+    gradient = gbuf[...]
     part = jnp.sum(
         readout * (slope_two * lapin_two + bend_two * curv2_s[...]), axis=1, keepdims=True
     ) + jnp.sum(gradient * gradient, axis=1, keepdims=True)
@@ -220,10 +249,21 @@
     total = msg[0, 0] + msg[0, 1]
     for k in range(1, nz):
         total = total + (msg[k, 0] + msg[k, 1])
-    out[2 * own:2 * own + 8, 0:128] = total
-    arrived(out.at[theirs, :], gs, gr)
+    amp_out[...] = total[0:1, :2 * own]
+    kin_out[...] = total[1:2, :2 * own]
+    arrived(grad_out.at[theirs, :], gs, gr)
+    keep.wait()
     for copy in sent:
         copy.wait_send()
+
+
+def hand_over(*refs):
+    sems = refs[-1]
+    copies = [pltpu.make_async_copy(refs[i], refs[3 + i], sems.at[i]) for i in range(3)]
+    for copy in copies:
+        copy.start()
+    for copy in copies:
+        copy.wait()
 
 
 def per_device(nw, nz, value_in, tang_in, lap_in, w_first, b_first, w_second, b_second, readout):
@@ -241,12 +281,14 @@
     chunks = own // CHUNK
     dma = pltpu.SemaphoreType.DMA
     in_hbm = pl.BlockSpec(memory_space=pltpu.HBM)
+    in_vmem = pl.BlockSpec(memory_space=pltpu.VMEM)
     rows = own * cols
-    out = pl.pallas_call(
+    row = jax.ShapeDtypeStruct((1, walkers), F32)
+    results = pl.pallas_call(
         functools.partial(kernel, nw, nz, gather),
-        out_shape=jax.ShapeDtypeStruct((walkers + 8, cols if cols > 128 else 128), F32),
+        out_shape=(jax.ShapeDtypeStruct((walkers, cols), F32), row, row),
         in_specs=[in_hbm] * 8,
-        out_specs=pl.BlockSpec(memory_space=pltpu.VMEM),
+        out_specs=(in_hbm, in_vmem, in_vmem),
         scratch_shapes=[
             pltpu.VMEM((own, cols, width), BF16),
             pltpu.VMEM(w_shape, BF16),
@@ -257,16 +299,21 @@
             pltpu.VMEM((own, width), F32),
             pltpu.VMEM((own, width), F32),
             pltpu.VMEM((own, width), F32),
+            pltpu.VMEM((own, cols), F32),
             pltpu.VMEM((nz, 2, 8, 128), F32),
-            dma((7 + chunks,)),
+            dma((8 + chunks,)),
             dma((2 + chunks,)),
             dma((2 + chunks,)),
             dma((2, nz)),
             dma((2, nz)),
-            dma((2, nz, nw)),
-            dma((2, nz, nw)),
-            dma((2, nz)),
-            dma((2, nz)),
+            dma((nz, nw)),
+            dma((nz, nw)),
+            dma((nz,)),
+            dma((nz,)),
+            dma((nw,)),
+            dma((nw,)),
+            dma((nw,)),
+            dma((nw,)),
             dma,
             dma,
             dma((nz, 2)),
@@ -282,7 +329,14 @@
         value_in, tang_in, lap_in, w_first, b_first.reshape(1, width),
         w_second, b_second.reshape(1, width), readout.reshape(1, width),
     )
-    return (out[walkers, :walkers], out[:walkers, :cols], out[walkers + 1, :walkers])
+    grad, amp, kin = pl.pallas_call(
+        hand_over,
+        out_shape=[jax.ShapeDtypeStruct(a.shape, a.dtype) for a in results],
+        in_specs=[in_hbm] * 3,
+        out_specs=[in_hbm] * 3,
+        scratch_shapes=[dma((3,))],
+    )(*results)
+    return (amp.reshape(walkers), grad, kin.reshape(walkers))
 
 
 def solution(mesh):

time: 32.2 us -> 30.9 us (0.960)
  local copies, waits for them, and re-layouts: 2.65 us -> 0 us
  Pallas kernels: 28.7 us -> 30 us
    slice x1 -> x0, local copies, waits for them, and re-layouts: 1.37 us -> none  [per_device(): out[:walkers, :cols]]
    pallas_call x1 -> x2, Pallas kernels: 28.7 us -> 30 us  [the longest x1 27.9 us: per_device(): pl.pallas_call(functools.partial(kernel, nw, nz, gather), out_shape=(jax....]
    squeeze x1 -> x0, local copies, waits for them, and re-layouts: 1.27 us -> none  [per_device(): out[walkers + 1, :walkers]]
where the time goes in v3:
time: 30.9 us; the launch traced here: 30.7 us
  Pallas kernels  30 us (97%)
  between operations  0.64 us (2%)
    pallas_call x1, Pallas kernels, per_device(): pl.pallas_call(functools.partial(kernel, nw, nz, gather), out_shape=(jax....  27.9 us
    pallas_call x1, Pallas kernels, per_device(): pl.pallas_call(hand_over, out_shape=[jax.ShapeDtypeStruct(a.shape, a.dtyp...  2.15 us

profile of v3, /device:TPU:0, one launch (start us, length us, event | category | flops | bytes accessed | tf_op | source)
XLA Modules:
  0.0 30.7 jit_solution(3036353796109984649)
XLA Ops:
  0.6 27.9 %shard_map.103 = (f32[32,192]{1,0:T(8,128)}, f32[1,32]{1,0:T(1,128)}, f32[1,32]{1,0:T(1,128)}) custom-call(bf16[32,256]{1,0:T(8,128)(2,1)} %value_ref.1, bf16[32,192,256]{2,1,0:T(8,128)(2,1)} %tang_ref.1, bf16[32,256]{1,0:T(8,128)(2,1)} %lap_ref.1, bf16[16,512]{1,0:T(8,128)(2,1)} %w1_ref.1, f32[1,512]{1,0:T(1,128)} %bitcast.5, bf16[16,512]{1,0:T(8,128)(2,1)} %w2_ref.1, ...), custom_call_target="tpu_custom_call" | custom-call | flops 3221225472 | bytes 3145728 | tf_op jit(solution)/shard_map/pallas_call | solution.py:287
  28.5 2.2 %shard_map.104 = (f32[32,192]{1,0:T(8,128)}, f32[1,32]{1,0:T(1,128)}, f32[1,32]{1,0:T(1,128)}) custom-call(f32[32,192]{1,0:T(8,128)} %get-tuple-element.9.refs_0_, f32[1,32]{1,0:T(1,128)} %get-tuple-element.10.refs_1_, f32[1,32]{1,0:T(1,128)} %get-tuple-element.11.refs_2_), custom_call_target="tpu_custom_call" | custom-call | tf_op jit(solution)/shard_map/pallas_call | solution.py:332

commit v4 on v3

--- a/solution.py
+++ b/solution.py
@@ -27,13 +27,14 @@
     nw, nz, gather,
     value_ref, tang_ref, lap_ref, w1_ref, b1_ref, w2_ref, b2_ref, r_ref,
     grad_out, amp_out, kin_out,
-    x, w1_all, w2_all, vl, vec, slope_s, weight_s, curv1_s, curv2_s, gbuf, msg,
+    x, x_two, w1_all, w2_all, vl, vec, slope_s, weight_s, curv1_s, curv2_s, gbuf, msg,
     loc, ps, pr, za_s, za_r, wb_s, wb_r, fc_s, fc_r, vb_s, vb_r, vc_s, vc_r, gs, gr, ms, mr,
 ):
     w, z, f = lax.axis_index("walker"), lax.axis_index("tangent"), lax.axis_index("feat")
     other = 1 - f
     own, cols, width = x.shape
     half = width // 2
+    parts = (slice(0, half), slice(half, width))
     chunks = own // CHUNK
     mine = pl.ds(pl.multiple_of(f * own, own), own)
     theirs = pl.ds(pl.multiple_of(other * own, own), own)
@@ -158,12 +159,12 @@
             if k < chunks:
                 give(k)
             pass_over(k - 1)
-        pass_over(nz - 1)
         for c in range(nz, chunks):
             give(c)
         for k in range(1, nz):
             from_z(1, k)
         second_across()
+        pass_over(nz - 1)
         second_over(0)
     else:
         for c in range(1, chunks):
@@ -188,12 +189,13 @@
         pltpu.make_async_copy(own_part, own_part, loc.at[tang_at + c]).wait()
         arrived(x.at[pl.ds(c * CHUNK, CHUNK), :, their_cols], ps.at[2 + c], pr.at[2 + c])
         block = x[pl.ds(c * CHUNK, CHUNK)].reshape(CHUNK * cols, width)
-        grad = dot(block, w1)
-        for i in range(CHUNK):
-            row = c * CHUNK + i
-            g = grad[i * cols:(i + 1) * cols]
-            curv1_s[pl.ds(row, 1), :] = jnp.sum(g * g, axis=0, keepdims=True)
-            x[row] = (slope_s[pl.ds(row, 1), :] * g).astype(BF16)
+        for part in parts:
+            grad = dot(block, w1[:, part])
+            for i in range(CHUNK):
+                row = c * CHUNK + i
+                g = grad[i * cols:(i + 1) * cols]
+                curv1_s[pl.ds(row, 1), part] = jnp.sum(g * g, axis=0, keepdims=True)
+                x_two[row, :, part] = (slope_s[pl.ds(row, 1), part] * g).astype(BF16)
         return carry
 
     lax.fori_loop(0, chunks - 1, first, 0)
@@ -213,15 +215,18 @@
     weight_s[...] = readout * slope_two
 
     def second(c, carry):
-        block = x[pl.ds(c * CHUNK, CHUNK)].reshape(CHUNK * cols, width)
-        grad = dot(block, w2)
+        block = x_two[pl.ds(c * CHUNK, CHUNK)].reshape(CHUNK * cols, width)
+        folded = [0.0] * CHUNK
+        for part in parts:
+            grad = dot(block, w2[:, part])
+            for i in range(CHUNK):
+                row = c * CHUNK + i
+                g = grad[i * cols:(i + 1) * cols]
+                curv2_s[pl.ds(row, 1), part] = jnp.sum(g * g, axis=0, keepdims=True)
+                terms = weight_s[pl.ds(row, 1), part] * g
+                folded[i] += sum(terms[:, j:j + 128] for j in range(0, terms.shape[1], 128))
         for i in range(CHUNK):
-            row = c * CHUNK + i
-            g = grad[i * cols:(i + 1) * cols]
-            curv2_s[pl.ds(row, 1), :] = jnp.sum(g * g, axis=0, keepdims=True)
-            terms = weight_s[pl.ds(row, 1), :] * g
-            terms = sum(terms[:, j:j + 128] for j in range(0, width, 128))
-            gbuf[pl.ds(row, 1), :] = jnp.sum(terms.T, axis=0, keepdims=True)
+            gbuf[pl.ds(c * CHUNK + i, 1), :] = jnp.sum(folded[i].T, axis=0, keepdims=True)
         return carry
 
     lax.fori_loop(0, chunks, second, 0)
@@ -259,10 +264,14 @@
 
 def hand_over(*refs):
     sems = refs[-1]
-    copies = [pltpu.make_async_copy(refs[i], refs[3 + i], sems.at[i]) for i in range(3)]
-    for copy in copies:
+    reads = [pltpu.make_async_copy(refs[i], refs[6 + i], sems.at[i]) for i in range(3)]
+    writes = [pltpu.make_async_copy(refs[6 + i], refs[3 + i], sems.at[3 + i]) for i in range(3)]
+    for copy in reads:
         copy.start()
-    for copy in copies:
+    for read, write in zip(reads, writes):
+        read.wait()
+        write.start()
+    for copy in writes:
         copy.wait()
 
 
@@ -290,6 +299,7 @@
         in_specs=[in_hbm] * 8,
         out_specs=(in_hbm, in_vmem, in_vmem),
         scratch_shapes=[
+            pltpu.VMEM((own, cols, width), BF16),
             pltpu.VMEM((own, cols, width), BF16),
             pltpu.VMEM(w_shape, BF16),
             pltpu.VMEM(w_shape, BF16),
@@ -334,7 +344,8 @@
         out_shape=[jax.ShapeDtypeStruct(a.shape, a.dtype) for a in results],
         in_specs=[in_hbm] * 3,
         out_specs=[in_hbm] * 3,
-        scratch_shapes=[dma((3,))],
+        scratch_shapes=[pltpu.VMEM(a.shape, a.dtype) for a in results] + [dma((6,))],
+        compiler_params=pltpu.CompilerParams(vmem_limit_bytes=64 * 2**20),
     )(*results)
     return (amp.reshape(walkers), grad, kin.reshape(walkers))
 

time: 30.9 us -> 29.3 us (0.948)
  Pallas kernels: 30 us -> 28.4 us
    pallas_call x1, Pallas kernels: 27.9 us -> 26.9 us  [per_device(): pl.pallas_call(functools.partial(kernel, nw, nz, gather), out_shape=(jax....]
    pallas_call x1, Pallas kernels: 2.15 us -> 1.43 us  [per_device(): pl.pallas_call(hand_over, out_shape=[jax.ShapeDtypeStruct(a.shape, a.dtyp...]
where the time goes in v4:
time: 29.3 us; the launch traced here: 29 us
  Pallas kernels  28.4 us (97%)
  between operations  0.64 us (2%)
    pallas_call x1, Pallas kernels, per_device(): pl.pallas_call(functools.partial(kernel, nw, nz, gather), out_shape=(jax....  26.9 us
    pallas_call x1, Pallas kernels, per_device(): pl.pallas_call(hand_over, out_shape=[jax.ShapeDtypeStruct(a.shape, a.dtyp...  1.43 us

profile of v4, /device:TPU:0, one launch (start us, length us, event | category | flops | bytes accessed | tf_op | source)
XLA Modules:
  0.0 29.0 jit_solution(12646754719872862089)
XLA Ops:
  0.6 26.9 %shard_map.103 = (f32[32,192]{1,0:T(8,128)}, f32[1,32]{1,0:T(1,128)}, f32[1,32]{1,0:T(1,128)}) custom-call(bf16[32,256]{1,0:T(8,128)(2,1)} %value_ref.1, bf16[32,192,256]{2,1,0:T(8,128)(2,1)} %tang_ref.1, bf16[32,256]{1,0:T(8,128)(2,1)} %lap_ref.1, bf16[16,512]{1,0:T(8,128)(2,1)} %w1_ref.1, f32[1,512]{1,0:T(1,128)} %bitcast.5, bf16[16,512]{1,0:T(8,128)(2,1)} %w2_ref.1, ...), custom_call_target="tpu_custom_call" | custom-call | flops 3221225472 | bytes 3145728 | tf_op jit(solution)/shard_map/pallas_call | solution.py:296
  27.6 1.4 %shard_map.104 = (f32[32,192]{1,0:T(8,128)}, f32[1,32]{1,0:T(1,128)}, f32[1,32]{1,0:T(1,128)}) custom-call(f32[32,192]{1,0:T(8,128)} %get-tuple-element.9.refs_0_, f32[1,32]{1,0:T(1,128)} %get-tuple-element.10.refs_1_, f32[1,32]{1,0:T(1,128)} %get-tuple-element.11.refs_2_), custom_call_target="tpu_custom_call" | custom-call | tf_op jit(solution)/shard_map/pallas_call | solution.py:342

commit v5 on v4

--- a/solution.py
+++ b/solution.py
@@ -28,7 +28,7 @@
     value_ref, tang_ref, lap_ref, w1_ref, b1_ref, w2_ref, b2_ref, r_ref,
     grad_out, amp_out, kin_out,
     x, x_two, w1_all, w2_all, vl, vec, slope_s, weight_s, curv1_s, curv2_s, gbuf, msg,
-    loc, ps, pr, za_s, za_r, wb_s, wb_r, fc_s, fc_r, vb_s, vb_r, vc_s, vc_r, gs, gr, ms, mr,
+    loc, ps, pr, za_s, za_r, wb_s, wb_r, wx_s, wx_r, fc_s, fc_r, vb_s, vb_r, vc_s, vc_r, gs, gr, ms, mr,
 ):
     w, z, f = lax.axis_index("walker"), lax.axis_index("tangent"), lax.axis_index("feat")
     other = 1 - f
@@ -42,11 +42,19 @@
     their_cols = pl.ds(pl.multiple_of(other * half, half), half)
     partner = (w, z, other)
 
+    def flipped(index, k):
+        bit = 1
+        while bit <= k:
+            if (k // bit) % 2:
+                index = index + bit - 2 * bit * lax.rem(lax.div(index, bit), 2)
+            bit *= 2
+        return index
+
     def z_at(k):
-        return lax.rem(z + k, nz)
+        return flipped(z, k)
 
     def w_at(k):
-        return lax.rem(w + k, nw)
+        return flipped(w, k)
 
     def remote(src, dst, send, recv, device):
         return pltpu.make_async_remote_copy(
@@ -76,7 +84,8 @@
     for k in range(1, nz):
         greeted += [(w, z_at(k), f), (w, z_at(k), other)]
     if gather:
-        greeted += [(w_at(k), z, f) for k in range(1, nw)]
+        for k in range(1, nw):
+            greeted += [(w_at(k), z, f), (w_at(k), z, other)]
     for device in greeted:
         pl.semaphore_signal(barrier, inc=1, device_id=device, device_id_type=MESH)
     if gather:
@@ -102,18 +111,22 @@
             send(piece, piece, za_s.at[layer, k], za_r.at[layer, k], (w, z_at(k), f))
 
     def from_z(layer, k):
-        arrived(weights[layer].at[w, z_at(nz - k), f], za_s.at[layer, k], za_r.at[layer, k])
+        arrived(weights[layer].at[w, z_at(k), f], za_s.at[layer, k], za_r.at[layer, k])
 
     def pass_across(k):
-        piece = w1_all.at[w, z_at(nz - k), f]
+        piece = w1_all.at[w, z_at(k), f]
         for j in range(1, nw):
             send(piece, piece, wb_s.at[k, j], wb_r.at[k, j], (w_at(j), z, f))
+        if k == nz - 1:
+            for j in range(nw):
+                send(piece, piece, wx_s.at[j], wx_r.at[j], (w_at(j), z, other))
 
     def pass_over(k):
         for j in range(1, nw):
-            arrived(w1_all.at[w_at(nw - j), z_at(nz - k), f], wb_s.at[k, j], wb_r.at[k, j])
-        piece = w1_all.at[:, z_at(nz - k), f]
-        send(piece, piece, fc_s.at[k], fc_r.at[k], partner)
+            arrived(w1_all.at[w_at(j), z_at(k), f], wb_s.at[k, j], wb_r.at[k, j])
+        if k < nz - 1:
+            piece = w1_all.at[:, z_at(k), f]
+            send(piece, piece, fc_s.at[k], fc_r.at[k], partner)
 
     def second_across():
         piece = w2_all.at[w, :, f]
@@ -121,7 +134,7 @@
             send(piece, piece, vb_s.at[j], vb_r.at[j], (w_at(j), z, f))
 
     def second_over(j):
-        piece = w2_all.at[w_at(nw - j), :, f]
+        piece = w2_all.at[w_at(j), :, f]
         if j:
             arrived(piece, vb_s.at[j], vb_r.at[j])
         send(piece, piece, vc_s.at[j], vc_r.at[j], partner)
@@ -131,11 +144,13 @@
         if not gather:
             own_w[layer].wait()
         elif layer == 0:
-            for k in range(nz):
-                arrived(dst.at[:, z_at(nz - k), other], fc_s.at[k], fc_r.at[k])
+            for k in range(nz - 1):
+                arrived(dst.at[:, z_at(k), other], fc_s.at[k], fc_r.at[k])
+            for j in range(nw):
+                arrived(dst.at[w_at(j), z_at(nz - 1), other], wx_s.at[j], wx_r.at[j])
         else:
             for j in range(nw):
-                arrived(dst.at[w_at(nw - j), :, other], vc_s.at[j], vc_r.at[j])
+                arrived(dst.at[w_at(j), :, other], vc_s.at[j], vc_r.at[j])
         return dst[...].reshape(width, width)
 
     def give(c):
@@ -250,7 +265,7 @@
     for k, g in others:
         send(slot, slot, ms.at[k, g], mr.at[k, g], (w, z_at(k), other if g else f))
     for k, g in others:
-        arrived(msg.at[z_at(nz - k), other if g else f], ms.at[k, g], mr.at[k, g])
+        arrived(msg.at[z_at(k), other if g else f], ms.at[k, g], mr.at[k, g])
     total = msg[0, 0] + msg[0, 1]
     for k in range(1, nz):
         total = total + (msg[k, 0] + msg[k, 1])
@@ -318,6 +333,8 @@
             dma((2, nz)),
             dma((nz, nw)),
             dma((nz, nw)),
+            dma((nw,)),
+            dma((nw,)),
             dma((nz,)),
             dma((nz,)),
             dma((nw,)),

time: 29.3 us -> 29 us (0.990)
  Pallas kernels: 28.4 us -> 28.1 us
where the time goes in v5:
time: 29 us; the launch traced here: 28.8 us
  Pallas kernels  28.1 us (97%)
  between operations  0.64 us (2%)
    pallas_call x1, Pallas kernels, per_device(): pl.pallas_call(functools.partial(kernel, nw, nz, gather), out_shape=(jax....  26.7 us
    pallas_call x1, Pallas kernels, per_device(): pl.pallas_call(hand_over, out_shape=[jax.ShapeDtypeStruct(a.shape, a.dtyp...  1.43 us

profile of v5, /device:TPU:0, one launch (start us, length us, event | category | flops | bytes accessed | tf_op | source)
XLA Modules:
  0.0 28.8 jit_solution(11391258304443704054)
XLA Ops:
  0.6 26.7 %shard_map.103 = (f32[32,192]{1,0:T(8,128)}, f32[1,32]{1,0:T(1,128)}, f32[1,32]{1,0:T(1,128)}) custom-call(bf16[32,256]{1,0:T(8,128)(2,1)} %value_ref.1, bf16[32,192,256]{2,1,0:T(8,128)(2,1)} %tang_ref.1, bf16[32,256]{1,0:T(8,128)(2,1)} %lap_ref.1, bf16[16,512]{1,0:T(8,128)(2,1)} %w1_ref.1, f32[1,512]{1,0:T(1,128)} %bitcast.5, bf16[16,512]{1,0:T(8,128)(2,1)} %w2_ref.1, ...), custom_call_target="tpu_custom_call" | custom-call | flops 3221225472 | bytes 3145728 | tf_op jit(solution)/shard_map/pallas_call | solution.py:311
  27.4 1.4 %shard_map.104 = (f32[32,192]{1,0:T(8,128)}, f32[1,32]{1,0:T(1,128)}, f32[1,32]{1,0:T(1,128)}) custom-call(f32[32,192]{1,0:T(8,128)} %get-tuple-element.9.refs_0_, f32[1,32]{1,0:T(1,128)} %get-tuple-element.10.refs_1_, f32[1,32]{1,0:T(1,128)} %get-tuple-element.11.refs_2_), custom_call_target="tpu_custom_call" | custom-call | tf_op jit(solution)/shard_map/pallas_call | solution.py:359

commit v6 on v5

--- a/solution.py
+++ b/solution.py
@@ -165,25 +165,20 @@
         pass_across(0)
     for i, src in enumerate((value_ref, lap_ref)):
         send(src.at[theirs, :], vl.at[i, :, my_cols], ps.at[i], pr.at[i], partner)
-    give(0)
     if gather:
         along_z(1)
+    for c in range(chunks):
+        give(c)
+    if gather:
         for k in range(1, nz):
             from_z(0, k)
             pass_across(k)
-            if k < chunks:
-                give(k)
             pass_over(k - 1)
-        for c in range(nz, chunks):
-            give(c)
         for k in range(1, nz):
             from_z(1, k)
         second_across()
         pass_over(nz - 1)
         second_over(0)
-    else:
-        for c in range(1, chunks):
-            give(c)
 
     for copy in own_vec + own_vl:
         copy.wait()

time: 29 us -> 29 us (level)
  no operation moved by 1% of the time
where the time goes in v6:
time: 29 us; the launch traced here: 28.8 us
  Pallas kernels  28.1 us (97%)
  between operations  0.64 us (2%)
    pallas_call x1, Pallas kernels, per_device(): pl.pallas_call(functools.partial(kernel, nw, nz, gather), out_shape=(jax....  26.7 us
    pallas_call x1, Pallas kernels, per_device(): pl.pallas_call(hand_over, out_shape=[jax.ShapeDtypeStruct(a.shape, a.dtyp...  1.43 us

profile of v6, /device:TPU:0, one launch (start us, length us, event | category | flops | bytes accessed | tf_op | source)
XLA Modules:
  0.0 28.8 jit_solution(2185678975103579149)
XLA Ops:
  0.6 26.7 %shard_map.103 = (f32[32,192]{1,0:T(8,128)}, f32[1,32]{1,0:T(1,128)}, f32[1,32]{1,0:T(1,128)}) custom-call(bf16[32,256]{1,0:T(8,128)(2,1)} %value_ref.1, bf16[32,192,256]{2,1,0:T(8,128)(2,1)} %tang_ref.1, bf16[32,256]{1,0:T(8,128)(2,1)} %lap_ref.1, bf16[16,512]{1,0:T(8,128)(2,1)} %w1_ref.1, f32[1,512]{1,0:T(1,128)} %bitcast.5, bf16[16,512]{1,0:T(8,128)(2,1)} %w2_ref.1, ...), custom_call_target="tpu_custom_call" | custom-call | flops 3221225472 | bytes 3145728 | tf_op jit(solution)/shard_map/pallas_call | solution.py:306
  27.4 1.4 %shard_map.104 = (f32[32,192]{1,0:T(8,128)}, f32[1,32]{1,0:T(1,128)}, f32[1,32]{1,0:T(1,128)}) custom-call(f32[32,192]{1,0:T(8,128)} %get-tuple-element.9.refs_0_, f32[1,32]{1,0:T(1,128)} %get-tuple-element.10.refs_1_, f32[1,32]{1,0:T(1,128)} %get-tuple-element.11.refs_2_), custom_call_target="tpu_custom_call" | custom-call | tf_op jit(solution)/shard_map/pallas_call | solution.py:354

commit v7 on v6

--- a/solution.py
+++ b/solution.py
@@ -10,7 +10,7 @@
 F32 = jnp.float32
 BF16 = jnp.bfloat16
 MESH = pl.DeviceIdType.MESH
-CHUNK = 4
+CHUNK = 8
 
 
 def dot(a, b):
@@ -235,16 +235,22 @@
                 curv2_s[pl.ds(row, 1), part] = jnp.sum(g * g, axis=0, keepdims=True)
                 terms = weight_s[pl.ds(row, 1), part] * g
                 folded[i] += sum(terms[:, j:j + 128] for j in range(0, terms.shape[1], 128))
+        terms = jnp.concatenate(folded, axis=0)
+        high = terms.astype(BF16)
+        low = (terms - high.astype(F32)).astype(BF16)
+        sums = dot(jnp.concatenate([high, low], axis=1), jnp.ones((256, 128), BF16))
         for i in range(CHUNK):
-            gbuf[pl.ds(c * CHUNK + i, 1), :] = jnp.sum(folded[i].T, axis=0, keepdims=True)
+            here = walker_lane == c * CHUNK + i
+            carry = carry + jnp.where(here, sums[i * cols:(i + 1) * cols], 0.0)
         return carry
 
-    lax.fori_loop(0, chunks, second, 0)
+    walker_lane = lax.broadcasted_iota(jnp.int32, (cols, 128), 1)
+    gradient = lax.fori_loop(0, chunks, second, jnp.zeros((cols, 128), F32)).T[:own]
+    gbuf[...] = gradient
 
     send(gbuf, grad_out.at[mine, :], gs, gr, partner)
     keep = pltpu.make_async_copy(gbuf, grad_out.at[mine, :], loc.at[len(local)])
     keep.start()
-    gradient = gbuf[...]
     part = jnp.sum(
         readout * (slope_two * lapin_two + bend_two * curv2_s[...]), axis=1, keepdims=True
     ) + jnp.sum(gradient * gradient, axis=1, keepdims=True)

time: 29 us -> 28.6 us (0.986)
  Pallas kernels: 28.1 us -> 27.7 us
    pallas_call x1, Pallas kernels: 26.7 us -> 26.3 us  [per_device(): pl.pallas_call(functools.partial(kernel, nw, nz, gather), out_shape=(jax....]
where the time goes in v7:
time: 28.6 us; the launch traced here: 28.3 us
  Pallas kernels  27.7 us (97%)
  between operations  0.64 us (2%)
    pallas_call x1, Pallas kernels, per_device(): pl.pallas_call(functools.partial(kernel, nw, nz, gather), out_shape=(jax....  26.3 us
    pallas_call x1, Pallas kernels, per_device(): pl.pallas_call(hand_over, out_shape=[jax.ShapeDtypeStruct(a.shape, a.dtyp...  1.43 us

profile of v7, /device:TPU:0, one launch (start us, length us, event | category | flops | bytes accessed | tf_op | source)
XLA Modules:
  0.0 28.3 jit_solution(10085696938170713211)
XLA Ops:
  0.6 26.3 %shard_map.103 = (f32[32,192]{1,0:T(8,128)}, f32[1,32]{1,0:T(1,128)}, f32[1,32]{1,0:T(1,128)}) custom-call(bf16[32,256]{1,0:T(8,128)(2,1)} %value_ref.1, bf16[32,192,256]{2,1,0:T(8,128)(2,1)} %tang_ref.1, bf16[32,256]{1,0:T(8,128)(2,1)} %lap_ref.1, bf16[16,512]{1,0:T(8,128)(2,1)} %w1_ref.1, f32[1,512]{1,0:T(1,128)} %bitcast.5, bf16[16,512]{1,0:T(8,128)(2,1)} %w2_ref.1, ...), custom_call_target="tpu_custom_call" | custom-call | flops 3221225472 | bytes 3145728 | tf_op jit(solution)/shard_map/pallas_call | solution.py:312
  26.9 1.4 %shard_map.104 = (f32[32,192]{1,0:T(8,128)}, f32[1,32]{1,0:T(1,128)}, f32[1,32]{1,0:T(1,128)}) custom-call(f32[32,192]{1,0:T(8,128)} %get-tuple-element.9.refs_0_, f32[1,32]{1,0:T(1,128)} %get-tuple-element.10.refs_1_, f32[1,32]{1,0:T(1,128)} %get-tuple-element.11.refs_2_), custom_call_target="tpu_custom_call" | custom-call | tf_op jit(solution)/shard_map/pallas_call | solution.py:360

commit v8 on v7

--- a/solution.py
+++ b/solution.py
@@ -10,7 +10,7 @@
 F32 = jnp.float32
 BF16 = jnp.bfloat16
 MESH = pl.DeviceIdType.MESH
-CHUNK = 8
+CHUNK = 4
 
 
 def dot(a, b):
@@ -173,10 +173,12 @@
         for k in range(1, nz):
             from_z(0, k)
             pass_across(k)
-            pass_over(k - 1)
+            if k < nz - 1:
+                pass_over(k - 1)
         for k in range(1, nz):
             from_z(1, k)
         second_across()
+        pass_over(nz - 2)
         pass_over(nz - 1)
         second_over(0)
 
@@ -208,11 +210,11 @@
                 x_two[row, :, part] = (slope_s[pl.ds(row, 1), part] * g).astype(BF16)
         return carry
 
-    lax.fori_loop(0, chunks - 1, first, 0)
+    lax.fori_loop(0, chunks // 2, first, 0)
     if gather:
         for j in range(1, nw):
             second_over(j)
-    first(chunks - 1, 0)
+    lax.fori_loop(chunks // 2, chunks, first, 0)
 
     w2 = whole(1)
     first_z = z == 0

time: 28.6 us -> 29.4 us (1.028)
  Pallas kernels: 27.7 us -> 28.5 us
    pallas_call x1, Pallas kernels: 26.3 us -> 27 us  [per_device(): pl.pallas_call(functools.partial(kernel, nw, nz, gather), out_shape=(jax....]
where the time goes in v8:
time: 29.4 us; the launch traced here: 29.1 us
  Pallas kernels  28.5 us (97%)
  between operations  0.64 us (2%)
    pallas_call x1, Pallas kernels, per_device(): pl.pallas_call(functools.partial(kernel, nw, nz, gather), out_shape=(jax....  27 us
    pallas_call x1, Pallas kernels, per_device(): pl.pallas_call(hand_over, out_shape=[jax.ShapeDtypeStruct(a.shape, a.dtyp...  1.43 us

profile of v8, /device:TPU:0, one launch (start us, length us, event | category | flops | bytes accessed | tf_op | source)
XLA Modules:
  0.0 29.1 jit_solution(7714399512448474985)
XLA Ops:
  0.6 27.0 %shard_map.103 = (f32[32,192]{1,0:T(8,128)}, f32[1,32]{1,0:T(1,128)}, f32[1,32]{1,0:T(1,128)}) custom-call(bf16[32,256]{1,0:T(8,128)(2,1)} %value_ref.1, bf16[32,192,256]{2,1,0:T(8,128)(2,1)} %tang_ref.1, bf16[32,256]{1,0:T(8,128)(2,1)} %lap_ref.1, bf16[16,512]{1,0:T(8,128)(2,1)} %w1_ref.1, f32[1,512]{1,0:T(1,128)} %bitcast.5, bf16[16,512]{1,0:T(8,128)(2,1)} %w2_ref.1, ...), custom_call_target="tpu_custom_call" | custom-call | flops 3221225472 | bytes 3145728 | tf_op jit(solution)/shard_map/pallas_call | solution.py:314
  27.7 1.4 %shard_map.104 = (f32[32,192]{1,0:T(8,128)}, f32[1,32]{1,0:T(1,128)}, f32[1,32]{1,0:T(1,128)}) custom-call(f32[32,192]{1,0:T(8,128)} %get-tuple-element.9.refs_0_, f32[1,32]{1,0:T(1,128)} %get-tuple-element.10.refs_1_, f32[1,32]{1,0:T(1,128)} %get-tuple-element.11.refs_2_), custom_call_target="tpu_custom_call" | custom-call | tf_op jit(solution)/shard_map/pallas_call | solution.py:362

commit v9 on v7

--- a/solution.py
+++ b/solution.py
@@ -186,6 +186,12 @@
         arrived(vl.at[i, :, their_cols], ps.at[i], pr.at[i])
     b1, b2, readout = vec[0], vec[1], vec[2]
 
+    def tangents_here(c):
+        own_part = x.at[pl.ds(c * CHUNK, CHUNK), :, my_cols]
+        pltpu.make_async_copy(own_part, own_part, loc.at[tang_at + c]).wait()
+        arrived(x.at[pl.ds(c * CHUNK, CHUNK), :, their_cols], ps.at[2 + c], pr.at[2 + c])
+
+    tangents_here(0)
     w1 = whole(0)
     vl_one = dot(vl[...].reshape(2 * own, width), w1)
     hidden_one = jnp.tanh(vl_one[:own] + b1)
@@ -194,10 +200,7 @@
     bend_one = -2.0 * hidden_one * slope_one
     slope_s[...] = slope_one
 
-    def first(c, carry):
-        own_part = x.at[pl.ds(c * CHUNK, CHUNK), :, my_cols]
-        pltpu.make_async_copy(own_part, own_part, loc.at[tang_at + c]).wait()
-        arrived(x.at[pl.ds(c * CHUNK, CHUNK), :, their_cols], ps.at[2 + c], pr.at[2 + c])
+    def first(c):
         block = x[pl.ds(c * CHUNK, CHUNK)].reshape(CHUNK * cols, width)
         for part in parts:
             grad = dot(block, w1[:, part])
@@ -206,13 +209,14 @@
                 g = grad[i * cols:(i + 1) * cols]
                 curv1_s[pl.ds(row, 1), part] = jnp.sum(g * g, axis=0, keepdims=True)
                 x_two[row, :, part] = (slope_s[pl.ds(row, 1), part] * g).astype(BF16)
-        return carry
-
-    lax.fori_loop(0, chunks - 1, first, 0)
+
+    for c in range(chunks - 1):
+        first(c)
+        tangents_here(c + 1)
     if gather:
         for j in range(1, nw):
             second_over(j)
-    first(chunks - 1, 0)
+    first(chunks - 1)
 
     w2 = whole(1)
     first_z = z == 0
@@ -245,7 +249,10 @@
         return carry
 
     walker_lane = lax.broadcasted_iota(jnp.int32, (cols, 128), 1)
-    gradient = lax.fori_loop(0, chunks, second, jnp.zeros((cols, 128), F32)).T[:own]
+    columns = jnp.zeros((cols, 128), F32)
+    for c in range(chunks):
+        columns = second(c, columns)
+    gradient = columns.T[:own]
     gbuf[...] = gradient
 
     send(gbuf, grad_out.at[mine, :], gs, gr, partner)

time: 28.6 us -> 28.3 us (0.990)
  Pallas kernels: 27.7 us -> 27.4 us
    pallas_call x1, Pallas kernels: 26.3 us -> 25.9 us  [per_device(): pl.pallas_call(functools.partial(kernel, nw, nz, gather), out_shape=(jax....]
where the time goes in v9:
time: 28.3 us; the launch traced here: 28 us
  Pallas kernels  27.4 us (97%)
  between operations  0.64 us (2%)
    pallas_call x1, Pallas kernels, per_device(): pl.pallas_call(functools.partial(kernel, nw, nz, gather), out_shape=(jax....  25.9 us
    pallas_call x1, Pallas kernels, per_device(): pl.pallas_call(hand_over, out_shape=[jax.ShapeDtypeStruct(a.shape, a.dtyp...  1.43 us

profile of v9, /device:TPU:0, one launch (start us, length us, event | category | flops | bytes accessed | tf_op | source)
XLA Modules:
  0.0 28.0 jit_solution(11328698963385577545)
XLA Ops:
  0.6 25.9 %shard_map.103 = (f32[32,192]{1,0:T(8,128)}, f32[1,32]{1,0:T(1,128)}, f32[1,32]{1,0:T(1,128)}) custom-call(bf16[32,256]{1,0:T(8,128)(2,1)} %value_ref.1, bf16[32,192,256]{2,1,0:T(8,128)(2,1)} %tang_ref.1, bf16[32,256]{1,0:T(8,128)(2,1)} %lap_ref.1, bf16[16,512]{1,0:T(8,128)(2,1)} %w1_ref.1, f32[1,512]{1,0:T(1,128)} %bitcast.5, bf16[16,512]{1,0:T(8,128)(2,1)} %w2_ref.1, ...), custom_call_target="tpu_custom_call" | custom-call | flops 3221225472 | bytes 3145728 | tf_op jit(solution)/shard_map/pallas_call | solution.py:319
  26.6 1.4 %shard_map.104 = (f32[32,192]{1,0:T(8,128)}, f32[1,32]{1,0:T(1,128)}, f32[1,32]{1,0:T(1,128)}) custom-call(f32[32,192]{1,0:T(8,128)} %get-tuple-element.9.refs_0_, f32[1,32]{1,0:T(1,128)} %get-tuple-element.10.refs_1_, f32[1,32]{1,0:T(1,128)} %get-tuple-element.11.refs_2_), custom_call_target="tpu_custom_call" | custom-call | tf_op jit(solution)/shard_map/pallas_call | solution.py:367
